TPU v7x, 256 devices: a whole 4x4x8 slice. The times are simulated.
256 devices in a mesh: dp: 4 (over x), row: 4 (over z_lo), col: 16 (over z_hi, y, core).
Axes of the slice: x: 4, y: 4, z: 8 (z_hi: 2, z_lo: 4; z = z_hi * 4 + z_lo), core: 2. Of those that a mesh axis runs over, the one named last changes fastest.
Arguments:
- outer_gate: bfloat16 [4, 8, 1024, 1024], P('dp', None, ('row', 'col')), may hold values from -6 to 6
- inner_gate: bfloat16 [4, 8, 1024, 1024], P('dp', None, ('row', 'col')), may hold values from -6 to 6
- signal: bfloat16 [4, 8, 1024, 1024], P('dp', None, ('row', 'col')), may hold values from -6 to 6
- grad_out: bfloat16 [4, 8, 1024, 1024], P('dp', None, ('row', 'col')), may hold values from -6 to 6
- filter_weight: float32 [1024, 1024], P(('row', 'col')), may hold values from -6 to 6
Outputs:
- grad_outer: bfloat16 [4, 8, 1024, 1024], P('dp', None, ('row', 'col'))
- grad_inner: bfloat16 [4, 8, 1024, 1024], P('dp', None, ('row', 'col'))
- grad_signal: bfloat16 [4, 8, 1024, 1024], P('dp', None, ('row', 'col'))
- grad_filter: float32 [1024, 1024], P(('row', 'col'))
All inputs are finite; a program needn't handle non-finite values.
Results may differ from a plain program's by a relative error of at most 0.0013.
Values sent between devices are 32-bit elements; how exact they have to be, the bound alone decides.
A program may use at most 128 MiB of HBM per device.

v0:
```python
import math

import jax
import jax.numpy as jnp
from jax import lax
from jax.sharding import PartitionSpec as P

TWO_PI = 2.0 * math.pi


def contract(form, left, right):
    return jnp.einsum(
        form, left, right, precision=lax.Precision.HIGHEST, preferred_element_type=jnp.float32
    )


def redistribute(blocks):
    return lax.all_to_all(blocks, ("row", "col"), split_axis=0, concat_axis=0, tiled=True)


def own_block():
    return lax.axis_index("row") * lax.axis_size("col") + lax.axis_index("col")


def turn_angles(first_index, second_index, total):
    product = first_index * second_index % total
    angles = product.astype(jnp.float32) * (TWO_PI / total)
    return (jnp.cos(angles), jnp.sin(angles))


def axis_dft(real, imag, sign):
    length, width = real.shape
    first = 1 << (length.bit_length() - 1) // 2
    second = length // first
    index_a = jnp.arange(first, dtype=jnp.int32)
    index_b = jnp.arange(second, dtype=jnp.int32)
    cos_a, sin_a = turn_angles(index_a[:, None], index_a[None, :], first)
    sin_a = sign * sin_a
    cos_b, sin_b = turn_angles(index_b[:, None], index_b[None, :], second)
    sin_b = sign * sin_b
    twist_cos, twist_sin = turn_angles(index_a[:, None], index_b[None, :], length)
    twist_cos = twist_cos[:, :, None]
    twist_sin = sign * twist_sin[:, :, None]
    real_three = real.reshape(first, second, width)
    step_real = contract("abm,ak->kbm", real_three, cos_a)
    step_imag = contract("abm,ak->kbm", real_three, sin_a)
    if imag is not None:
        imag_three = imag.reshape(first, second, width)
        step_real = step_real - contract("abm,ak->kbm", imag_three, sin_a)
        step_imag = step_imag + contract("abm,ak->kbm", imag_three, cos_a)
    turned_real = step_real * twist_cos - step_imag * twist_sin
    turned_imag = step_real * twist_sin + step_imag * twist_cos
    out_real = contract("kbm,bj->jkm", turned_real, cos_b) - contract(
        "kbm,bj->jkm", turned_imag, sin_b
    )
    out_imag = contract("kbm,bj->jkm", turned_real, sin_b) + contract(
        "kbm,bj->jkm", turned_imag, cos_b
    )
    return (out_real.reshape(length, width), out_imag.reshape(length, width))


def forward(stacked, order):
    count, block, grid_side = stacked.shape
    owners = grid_side // block
    total = grid_side * grid_side
    send = jnp.transpose(stacked.reshape(count, block, owners, block), (2, 1, 0, 3)).reshape(
        owners, block, count * block
    )
    columns = redistribute(send).reshape(grid_side, count * block)
    first_real, first_imag = axis_dft(columns, None, -1.0)
    first_real = first_real.reshape(grid_side, count, block)
    first_imag = first_imag.reshape(grid_side, count, block)
    col_index = own_block() * block + jnp.arange(block, dtype=jnp.int32)
    cos_turn, sin_turn = turn_angles(order[:, None, None], col_index[None, None, :], total)
    turned_real = first_real * cos_turn + first_imag * sin_turn
    turned_imag = first_imag * cos_turn - first_real * sin_turn
    send_two = jnp.concatenate([turned_real, turned_imag], axis=1).reshape(
        owners, block, 2 * count * block
    )
    gotten = redistribute(send_two).reshape(owners, block, 2 * count, block)
    flat_real = jnp.transpose(gotten[:, :, :count, :], (0, 3, 1, 2)).reshape(
        grid_side, block * count
    )
    flat_imag = jnp.transpose(gotten[:, :, count:, :], (0, 3, 1, 2)).reshape(
        grid_side, block * count
    )
    out_real, out_imag = axis_dft(flat_real, flat_imag, -1.0)
    spec_real = jnp.transpose(out_real.reshape(grid_side, block, count), (1, 2, 0))
    spec_imag = jnp.transpose(out_imag.reshape(grid_side, block, count), (1, 2, 0))
    return (spec_real, spec_imag)


def inverse(spec_real, spec_imag, order):
    block, count, grid_side = spec_real.shape
    owners = grid_side // block
    total = grid_side * grid_side
    flat_real = jnp.transpose(spec_real, (2, 0, 1)).reshape(grid_side, block * count)
    flat_imag = jnp.transpose(spec_imag, (2, 0, 1)).reshape(grid_side, block * count)
    out_real, out_imag = axis_dft(flat_real, flat_imag, 1.0)
    back_real = jnp.transpose(out_real.reshape(owners, block, block, count), (0, 2, 3, 1))
    back_imag = jnp.transpose(out_imag.reshape(owners, block, block, count), (0, 2, 3, 1))
    freq_index = lax.dynamic_slice_in_dim(order, own_block() * block, block, 0)
    col_index = (
        jnp.arange(owners, dtype=jnp.int32)[:, None] * block
        + jnp.arange(block, dtype=jnp.int32)[None, :]
    )
    cos_turn, sin_turn = turn_angles(
        freq_index[None, :, None, None], col_index[:, None, None, :], total
    )
    turned_real = back_real * cos_turn - back_imag * sin_turn
    turned_imag = back_real * sin_turn + back_imag * cos_turn
    send = jnp.concatenate([turned_real, turned_imag], axis=2).reshape(
        owners, block, 2 * count * block
    )
    gotten = redistribute(send).reshape(grid_side, 2 * count * block)
    real_part = gotten[:, : count * block]
    imag_part = gotten[:, count * block :]
    full_real, full_imag = axis_dft(real_part, imag_part, 1.0)
    values = full_real * (1.0 / total)
    returned = redistribute(values.reshape(owners, block, count * block)).reshape(
        owners, block, count, block
    )
    return jnp.transpose(returned, (2, 1, 0, 3)).reshape(count, block, grid_side)


def shards(outer_gate, inner_gate, signal, grad_out, filter_weight):
    grid_side = filter_weight.shape[1]
    freq_index = jnp.arange(grid_side, dtype=jnp.int32)
    outer_f = outer_gate[0].astype(jnp.float32)
    inner_f = inner_gate[0].astype(jnp.float32)
    signal_f = signal[0].astype(jnp.float32)
    grad_f = grad_out[0].astype(jnp.float32)
    channels = inner_f.shape[0]
    gated = inner_f * signal_f
    grad_conv = grad_f * outer_f
    taps = (filter_weight * (1.0 / grid_side))[None]
    spec_real, spec_imag = forward(jnp.concatenate([gated, grad_conv], axis=0), freq_index)
    filt_real, filt_imag = forward(taps, freq_index)
    gated_real = spec_real[:, :channels]
    gated_imag = spec_imag[:, :channels]
    cot_real = spec_real[:, channels : 2 * channels]
    cot_imag = spec_imag[:, channels : 2 * channels]
    conv_real = filt_real * gated_real - filt_imag * gated_imag
    conv_imag = filt_real * gated_imag + filt_imag * gated_real
    back_real = filt_real * cot_real + filt_imag * cot_imag
    back_imag = filt_real * cot_imag - filt_imag * cot_real
    term_real = jnp.sum(gated_real * cot_real + gated_imag * cot_imag, axis=1, keepdims=True)
    term_imag = jnp.sum(gated_real * cot_imag - gated_imag * cot_real, axis=1, keepdims=True)
    values = inverse(
        jnp.concatenate([conv_real, back_real, term_real], axis=1),
        jnp.concatenate([conv_imag, back_imag, term_imag], axis=1),
        freq_index,
    )
    grad_filter = lax.psum(values[2 * channels], "dp") * (1.0 / grid_side)
    conv = values[:channels]
    grad_gated = values[channels : 2 * channels]
    grad_outer = (grad_f * conv).astype(jnp.bfloat16)[None]
    grad_inner = (grad_gated * signal_f).astype(jnp.bfloat16)[None]
    grad_signal = (grad_gated * inner_f).astype(jnp.bfloat16)[None]
    return (grad_outer, grad_inner, grad_signal, grad_filter)


def solution(mesh):
    placed = (
        P("dp", None, ("row", "col"), None),
        P("dp", None, ("row", "col"), None),
        P("dp", None, ("row", "col"), None),
        P("dp", None, ("row", "col"), None),
        P(("row", "col"), None),
    )
    return jax.shard_map(
        shards,
        mesh=mesh,
        in_specs=placed,
        out_specs=(
            P("dp", None, ("row", "col"), None),
            P("dp", None, ("row", "col"), None),
            P("dp", None, ("row", "col"), None),
            P(("row", "col"), None),
        ),
        check_vma=False,
    )
```

profile of v0, /device:TPU:1, one launch (start us, length us, event | category | flops | bytes accessed | tf_op | source)
XLA Modules:
  0.0 529.6 jit_solution(14472906551521814959)
XLA Ops:
  9.5 13.2 %all-to-all-start = ((f32[64,1,256]{2,1,0:T(1,128)}), f32[64,1,256]{2,1,0:T(1,128)S(1)}, u32[]{:S(2)}, u32[]{:S(2)}) async-start(f32[64,1,256]{2,1,0:T(1,128)} %reshape.384), calls=%async_computation | async-start | bytes 131072 | tf_op jit(solution)/shard_map/all_to_all | solution.py:18
  41.3 10.2 %all-to-all-start.2 = ((f32[64,16,256]{2,1,0:T(8,128)}), f32[64,16,256]{2,1,0:T(8,128)S(1)}, u32[]{:S(2)}, u32[]{:S(2)}) async-start(f32[64,16,256]{2,1,0:T(8,128)} %copy.142), calls=%async_computation.2 | async-start | bytes 2097152 | tf_op jit(solution)/shard_map/all_to_all | solution.py:18
  62.5 17.9 %all-to-all-done.2 = f32[64,16,256]{2,1,0:T(8,128)S(1)} async-done(((f32[64,16,256]{2,1,0:T(8,128)}), f32[64,16,256]{2,1,0:T(8,128)S(1)}, u32[]{:S(2)}, u32[]{:S(2)}) %all-to-all-start.2) | async-done | bytes 1048608 | tf_op jit(solution)/shard_map/all_to_all | solution.py:18
  80.4 5.5 %all-to-all-start.1 = ((f32[64,1,512]{2,1,0:T(1,128)}), f32[64,1,512]{2,1,0:T(1,128)S(1)}, u32[]{:S(2)}, u32[]{:S(2)}) async-start(f32[64,1,512]{2,1,0:T(1,128)} %reshape.386), calls=%async_computation.1 | async-start | bytes 262144 | tf_op jit(solution)/shard_map/all_to_all | solution.py:18
  95.7 4.4 copy.150
  100.1 3.9 reshape_reshape.62
  104.1 4.4 copy.147
  112.7 9.0 %reshape.383 = f32[64,16,512]{1,0,2:T(8,128)} reshape(f32[1024,32,16]{0,2,1:T(8,128)S(1)} %pad_maximum_fusion.1) | data formatting | bytes 4194304 | tf_op jit(solution)/shard_map/reshape | solution.py:77
  121.7 10.8 %copy.189 = f32[64,16,512]{2,1,0:T(8,128)} copy(f32[64,16,512]{1,0,2:T(8,128)} %reshape.383) | data formatting | bytes 4194304 | tf_op jit(solution)/shard_map/reshape | solution.py:77
  132.5 10.2 %all-to-all-start.3 = ((f32[64,16,512]{2,1,0:T(8,128)}), f32[64,16,512]{2,1,0:T(8,128)S(1)}, u32[]{:S(2)}, u32[]{:S(2)}) async-start(f32[64,16,512]{2,1,0:T(8,128)} %copy.189), calls=%async_computation.3 | async-start | bytes 4194304 | tf_op jit(solution)/shard_map/all_to_all | solution.py:18
  157.5 36.3 %all-to-all-done.3 = f32[64,16,512]{2,1,0:T(8,128)S(1)} async-done(((f32[64,16,512]{2,1,0:T(8,128)}), f32[64,16,512]{2,1,0:T(8,128)S(1)}, u32[]{:S(2)}, u32[]{:S(2)}) %all-to-all-start.3) | async-done | bytes 2097184 | tf_op jit(solution)/shard_map/all_to_all | solution.py:18
  196.6 4.0 slice_bitcast_fusion
  200.6 8.6 %copy.153 = f32[64,16,16,16]{3,2,1,0:T(8,128)} copy(f32[64,16,16,16]{0,1,3,2:T(8,128)} %get-tuple-element.9) | data formatting | bytes 2097152 | tf_op jit(solution)/shard_map/transpose | solution.py:81
  209.2 6.6 %reshape_reshape.63 = f32[32,32,256]{2,1,0:T(8,128)S(1)} reshape(f32[64,16,16,16]{3,2,1,0:T(8,128)} %copy.153) | data formatting | bytes 2097152 | tf_op jit(solution)/shard_map/reshape;reshape | solution.py:44
  221.0 7.7 %copy.155 = f32[64,16,16,16]{3,2,1,0:T(8,128)} copy(f32[64,16,16,16]{0,1,3,2:T(8,128)S(1)} %get-tuple-element.8) | data formatting | bytes 2097152 | tf_op jit(solution)/shard_map/transpose | solution.py:84
  228.8 6.4 %reshape_reshape.64 = f32[32,32,256]{2,1,0:T(8,128)S(1)} reshape(f32[64,16,16,16]{3,2,1,0:T(8,128)} %copy.155) | data formatting | bytes 2097152 | tf_op jit(solution)/shard_map/reshape;reshape | solution.py:48
  245.2 4.4 copy.164
  249.6 3.9 reshape_reshape.67
  253.5 4.4 copy.161
  266.3 4.0 copy.165
  277.7 4.4 copy.166
  296.9 6.6 %reshape_reshape.70 = f32[64,16,16,17]{3,2,1,0:T(8,128)} reshape(f32[32,32,272]{2,1,0:T(8,128)S(1)} %copy.171) | data formatting | bytes 2228224 | tf_op jit(solution)/shard_map/reshape;reshape | solution.py:100
  303.5 6.6 %reshape_reshape.71 = f32[64,16,16,17]{3,2,1,0:T(8,128)} reshape(f32[32,32,272]{2,1,0:T(8,128)S(1)} %copy.174) | data formatting | bytes 2228224 | tf_op jit(solution)/shard_map/reshape;reshape | solution.py:101
  310.1 12.9 %fusion = (f32[64,16,17,16]{2,1,3,0:T(8,128)}, f32[64,16,17,16]{2,1,3,0:T(8,128)}) fusion(f32[64,16,16,17]{3,2,1,0:T(8,128)} %reshape_reshape.71, f32[64,16,16,17]{3,2,1,0:T(8,128)} %reshape_reshape.70, f32[64,16,16]{1,2,0:T(8,128)S(1)} %copy-done.5, f32[64,16,16]{1,2,0:T(8,128)S(1)} %copy-done.4), kind=kLoop, calls=%fused_computation.3 | loop fusion | flops 1671168 | bytes 4587520 | tf_op jit(solution)/shard_map/sub | solution.py:110
  323.0 11.2 %pad_maximum_fusion = f32[64,16,34,16]{2,1,3,0:T(8,128)} fusion(f32[64,16,17,16]{2,1,3,0:T(8,128)} %get-tuple-element.7, f32[64,16,17,16]{2,1,3,0:T(8,128)} %get-tuple-element.6), kind=kLoop, calls=%fused_computation | loop fusion | flops 557056 | bytes 4456448 | tf_op jit(solution)/shard_map/concatenate | solution.py:112
  334.2 8.3 %copy.175 = f32[64,16,34,16]{0,3,2,1:T(8,128)} copy(f32[64,16,34,16]{2,1,3,0:T(8,128)} %pad_maximum_fusion) | data formatting | bytes 4456448 | tf_op jit(solution)/shard_map/concatenate | solution.py:112
  342.5 4.3 copy.176
  346.8 67.7 %all_to_all.30 = f32[64,16,544]{2,1,0:T(8,128)S(1)} all-to-all(f32[64,16,544]{2,1,0:T(8,128)S(1)} %copy.176), channel_id=1, replica_groups=mesh['dp'=4,'row'=4,'col'=16] {'row','col'}, dimensions={0} | all-to-all | bytes 4456448 | tf_op jit(solution)/shard_map/all_to_all | solution.py:18
  430.6 45.8 %all_to_all.31 = f32[64,16,272]{2,1,0:T(8,128)} all-to-all(f32[64,16,272]{2,1,0:T(8,128)S(1)} %bitcast.215), channel_id=1, replica_groups=mesh['dp'=4,'row'=4,'col'=16] {'row','col'}, dimensions={0} | all-to-all | bytes 2228224 | tf_op jit(solution)/shard_map/all_to_all | solution.py:18
  483.5 4.8 slice.59
  491.9 4.7 slice.57
  497.4 23.4 %all-reduce.2.cloned.1.call-done = f32[16,1024]{1,0:T(8,128)} async-done(((f32[16,1024]{1,0:T(8,128)}), f32[16,1024]{1,0:T(8,128)}) %all-reduce.2.cloned.1.call-update) | async-done | bytes 65552 | tf_op jit(solution)/shard_map/psum | solution.py:154
  (147 shorter events, 137.9 us)
Async XLA Ops:
  7.2 15.5 %copy-start.8 = (bf16[1,8,16,1024]{3,2,1,0:T(8,128)(2,1)S(1)}, bf16[1,8,16,1024]{3,2,1,0:T(8,128)(2,1)}, u32[]{:S(2)}) copy-start(bf16[1,8,16,1024]{3,2,1,0:T(8,128)(2,1)} %param.7) | copy-start | bytes 786436
  7.2 15.5 %copy-start.10 = (bf16[1,8,16,1024]{3,2,1,0:T(8,128)(2,1)S(1)}, bf16[1,8,16,1024]{3,2,1,0:T(8,128)(2,1)}, u32[]{:S(2)}) copy-start(bf16[1,8,16,1024]{3,2,1,0:T(8,128)(2,1)} %param.6) | copy-start | bytes 786436
  9.5 31.8 %all-to-all-start = ((f32[64,1,256]{2,1,0:T(1,128)}), f32[64,1,256]{2,1,0:T(1,128)S(1)}, u32[]{:S(2)}, u32[]{:S(2)}) async-start(f32[64,1,256]{2,1,0:T(1,128)} %reshape.384), calls=%async_computation | async-start | bytes 131072 | tf_op jit(solution)/shard_map/all_to_all | solution.py:18
  25.5 2.9 copy-start.12
  25.5 2.9 copy-start.14
  41.3 39.1 %all-to-all-start.2 = ((f32[64,16,256]{2,1,0:T(8,128)}), f32[64,16,256]{2,1,0:T(8,128)S(1)}, u32[]{:S(2)}, u32[]{:S(2)}) async-start(f32[64,16,256]{2,1,0:T(8,128)} %copy.142), calls=%async_computation.2 | async-start | bytes 2097152 | tf_op jit(solution)/shard_map/all_to_all | solution.py:18
  80.4 52.1 %all-to-all-start.1 = ((f32[64,1,512]{2,1,0:T(1,128)}), f32[64,1,512]{2,1,0:T(1,128)S(1)}, u32[]{:S(2)}, u32[]{:S(2)}) async-start(f32[64,1,512]{2,1,0:T(1,128)} %reshape.386), calls=%async_computation.1 | async-start | bytes 262144 | tf_op jit(solution)/shard_map/all_to_all | solution.py:18
  132.5 61.3 %all-to-all-start.3 = ((f32[64,16,512]{2,1,0:T(8,128)}), f32[64,16,512]{2,1,0:T(8,128)S(1)}, u32[]{:S(2)}, u32[]{:S(2)}) async-start(f32[64,16,512]{2,1,0:T(8,128)} %copy.189), calls=%async_computation.3 | async-start | bytes 4194304 | tf_op jit(solution)/shard_map/all_to_all | solution.py:18
  142.7 378.1 %all-reduce.2.cloned.1.call-start = ((), (), s32[]{:S(2)}) async-start(), calls=%async_computation.6 | async-start | bytes 131072 | tf_op jit(solution)/shard_map/psum | solution.py:154
  228.8 6.4 %copy-start.2 = (f32[32,32,256]{2,0,1:T(8,128)S(1)}, f32[32,32,256]{2,0,1:T(8,128)}, u32[]{:S(2)}) copy-start(f32[32,32,256]{2,0,1:T(8,128)} %fusion.30) | copy-start | bytes 3145732
  235.2 1.6 copy-start.1
  273.0 1.6 copy-start.6
  273.0 1.6 copy-start.7
  282.1 1.6 copy-start
  303.5 6.6 %copy-start.4 = (f32[64,16,16]{1,2,0:T(8,128)S(1)}, f32[64,16,16]{1,2,0:T(8,128)}, u32[]{:S(2)}) copy-start(f32[64,16,16]{1,2,0:T(8,128)} %get-tuple-element.36) | copy-start | bytes 196612
  303.5 6.6 %copy-start.5 = (f32[64,16,16]{1,2,0:T(8,128)S(1)}, f32[64,16,16]{1,2,0:T(8,128)}, u32[]{:S(2)}) copy-start(f32[64,16,16]{1,2,0:T(8,128)} %get-tuple-element.37) | copy-start | bytes 196612
  479.7 1.2 copy-start.3
  483.5 4.8 copy-start.9
  483.5 4.8 copy-start.11
  491.9 4.8 copy-start.13
Sparse Core Ops, SparseCore 0:
  480.9 39.8 all-reduce.1
where the time goes:
time: 540 us; the launch traced here: 530 us
  local copies, waits for them, and re-layouts  176 us (33%)
  blocking collectives  113 us (21%)
  waiting for transfers between devices  77.6 us (14%)
  matrix products  70 us (13%)
  starting transfers between devices  39 us (7%)
  other arithmetic  38.2 us (7%)
  between operations  15.3 us (3%)
    all_to_all x2, blocking collectives, redistribute(): lax.all_to_all(blocks, ('row', 'col'), split_axis=0, concat_axis=0, tiled...  113 us
    dot_general x42, matrix products, contract(): jnp.einsum(form, left, right, precision=lax.Precision.HIGHEST, preferred_...  70 us
    all_to_all x4, waiting for transfers between devices, redistribute(): lax.all_to_all(blocks, ('row', 'col'), split_axis=0, concat_axis=0, tiled...  54.2 us
    all_to_all x4, starting transfers between devices, redistribute(): lax.all_to_all(blocks, ('row', 'col'), split_axis=0, concat_axis=0, tiled...  39 us
    psum x1, waiting for transfers between devices, shards(): grad_filter = lax.psum(values[2 * channels], 'dp') * (1.0 / grid_side)  23.4 us
    reshape x4, local copies, waits for them, and re-layouts, forward(): jnp.concatenate([turned_real, turned_imag], axis=1)  20.8 us
    another operation x5, local copies, waits for them, and re-layouts, axis_dft(): real_three = real.reshape(first, second, width)  13.8 us
    another operation x4, local copies, waits for them, and re-layouts, axis_dft(): imag_three = imag.reshape(first, second, width)  13.8 us
  transfers between devices with their start and end apart: 5, of which 3 were waited for; matrix products, arithmetic and copies ran while one was open for 20% of the time, Pallas kernels for 0%

commit v1 on v0

v1 whole, which is shorter than its diff:
```python
import functools
import math

import jax
import jax.numpy as jnp
import ml_dtypes
import numpy as np
from jax import lax
from jax.experimental import pallas as pl
from jax.experimental.pallas import tpu as pltpu
from jax.sharding import PartitionSpec as P

MESH = pl.DeviceIdType.MESH
F32 = jnp.float32
BF16 = jnp.bfloat16

SIDE = 1024
HALF = SIDE // 2
ROWS = 16
ZS = 8
SLABS = 8
LANES = SIDE // SLABS
KROWS = HALF // SLABS
RADIX = 4
QUARTER = SIDE // RADIX
PAD = KROWS + 8
ARRAYS = 3
KBLOCK = 2 * KROWS


def split_np(matrix):
    high = matrix.astype(np.float32).astype(ml_dtypes.bfloat16)
    low = (matrix - high.astype(np.float64)).astype(np.float32).astype(ml_dtypes.bfloat16)
    return np.stack([high, low])


def tables():
    side = np.arange(SIDE)
    half = np.arange(HALF)
    angle = 2 * np.pi * ((half[:, None] * side[None, :]) % SIDE) / SIDE
    cos, sin = np.cos(angle), np.sin(angle)
    sin[0] = (-1.0) ** side
    blocks = []
    for at in range(0, HALF, KBLOCK):
        blocks += [cos[at : at + KBLOCK], sin[at : at + KBLOCK]]
    rows_in = np.concatenate(blocks, axis=0)
    weight = np.where(half == 0, 0.5, 1.0)[:, None]
    rows_out = np.concatenate([cos * weight, -sin * weight], axis=0).T
    quarter = np.arange(QUARTER)
    small = 2 * np.pi * ((quarter[:, None] * quarter[None, :]) % QUARTER) / QUARTER
    cos_q, sin_q = np.cos(small), np.sin(small)
    cols_in = np.block([[cos_q, -sin_q], [sin_q, cos_q]])
    cols_out = np.block([[cos_q, sin_q], [-sin_q, cos_q]])
    total = SIDE * SIDE
    turn = 2 * np.pi * ((half[:, None] * side[None, :]) % total) / total
    turn = np.stack([np.cos(turn), np.sin(turn)]).reshape(2, HALF, SLABS, LANES)
    turn = np.transpose(turn, (2, 0, 1, 3)).astype(np.float32)
    twist = 2 * np.pi * np.arange(RADIX)[:, None] * quarter[None, :] / SIDE
    twist = np.concatenate([np.cos(twist), np.sin(twist)], axis=0).astype(np.float32)
    shift = np.pi * side / SIDE
    shift = np.stack([np.cos(shift), np.sin(shift)] * 4).astype(np.float32)
    return (
        split_np(rows_in),
        split_np(rows_out),
        split_np(cols_in),
        split_np(cols_out),
        turn,
        twist,
        shift,
    )


def split(value):
    high = value.astype(BF16)
    return high, (value - high.astype(F32)).astype(BF16)


def dot(left, right):
    return jnp.dot(left, right, preferred_element_type=F32)


def kernel(
    outer_ref, inner_ref, signal_ref, grad_ref, taps_ref, twist_ref, shift_ref,
    rows_in_hbm, rows_out_hbm, cols_in_hbm, cols_out_hbm, turn_hbm,
    d_outer_ref, d_inner_ref, d_signal_ref, d_taps_ref,
    rows_in, rows_out, cols_in, cols_out, turn,
    gated, cotangent, got_a, send_b, got_b, spec, send_c, got_c, done, got_d, part, got_e,
    halves, const_sem, send_sem, recv_sem,
):
    x = lax.axis_index("dp")
    row = lax.axis_index("row")
    col = lax.axis_index("col")
    rows_n = lax.axis_size("row")
    slab = lax.rem(col, SLABS)
    z = (col // SLABS) * rows_n + row
    block = row * lax.axis_size("col") + col

    def place(z_to, slab_to):
        return {"row": lax.rem(z_to, rows_n), "col": (z_to // rows_n) * SLABS + slab_to}

    consts = [
        pltpu.make_async_copy(source, target, const_sem.at[i])
        for i, (source, target) in enumerate(
            [
                (rows_in_hbm, rows_in),
                (turn_hbm.at[slab], turn),
                (cols_in_hbm, cols_in),
                (cols_out_hbm, cols_out),
                (rows_out_hbm, rows_out),
            ]
        )
    ]
    for copy in consts:
        copy.start()

    barrier = pltpu.get_barrier_semaphore()

    def partner(i):
        return lax.rem(z + i // SLABS, ZS), lax.rem(slab + lax.rem(i, SLABS), SLABS)

    def greet(i, carry):
        pl.semaphore_signal(barrier, inc=1, device_id=place(*partner(i)), device_id_type=MESH)
        return carry

    lax.fori_loop(1, ZS * SLABS, greet, 0)
    dps = lax.axis_size("dp")
    for i in range(1, dps):
        pl.semaphore_signal(
            barrier, inc=1, device_id={"dp": lax.rem(x + i, dps)}, device_id_type=MESH
        )

    gated[...] = inner_ref[...].astype(F32) * signal_ref[...].astype(F32)
    cotangent[...] = grad_ref[...].astype(F32) * outer_ref[...].astype(F32)
    pl.semaphore_wait(barrier, ZS * SLABS - 1 + dps - 1)

    def lane_slab(at):
        return pl.ds(pl.multiple_of(at * LANES, LANES), LANES)

    def row_block(at):
        return pl.ds(pl.multiple_of(at * ROWS, ROWS), ROWS)

    def k_rows(at):
        return pl.ds(pl.multiple_of(at * KROWS, KROWS), KROWS)

    def send_a(a, source_of):
        target = got_a.at[a, row_block(block)]
        pltpu.make_async_copy(source_of(z, slab), target, recv_sem.at[0, a]).start()

        def step(i, carry):
            z_to, slab_to = partner(i)
            pltpu.make_async_remote_copy(
                src_ref=source_of(z_to, slab_to), dst_ref=target,
                send_sem=send_sem.at[0, a], recv_sem=recv_sem.at[0, a],
                device_id=place(z_to, slab_to), device_id_type=MESH,
            ).start()
            return carry

        lax.fori_loop(1, ZS * SLABS, step, 0)

    send_a(0, lambda z_to, slab_to: taps_ref.at[:, lane_slab(slab_to)])
    send_a(1, lambda z_to, slab_to: gated.at[z_to, :, lane_slab(slab_to)])
    send_a(2, lambda z_to, slab_to: cotangent.at[z_to, :, lane_slab(slab_to)])

    def rows_forward(a):
        pltpu.make_async_copy(got_a.at[a], got_a.at[a], recv_sem.at[0, a]).wait()
        high, low = split(got_a[a])
        halves[:, :LANES] = high
        halves[:, LANES:] = low

        def step(i, carry):
            pair = lax.rem(slab // 2 + i, SLABS // 2)
            at = pl.ds(pl.multiple_of(pair * 2 * KBLOCK, 2 * KBLOCK), 2 * KBLOCK)
            wide = dot(rows_in[0, at], halves[...])
            both = wide[:, :LANES] + wide[:, LANES:] + dot(rows_in[1, at], halves[:, :LANES])
            even, odd = both[:KBLOCK], both[KBLOCK:]
            at = pl.ds(pl.multiple_of(pair * KBLOCK, KBLOCK), KBLOCK)
            cos, sin = turn[0, at], turn[1, at]
            real = even * cos - odd * sin
            imag = -(even * sin + odd * cos)
            for j in range(2):
                part_of = slice(j * KROWS, (j + 1) * KROWS)
                slab_to = pair * 2 + j
                send_b[a, slab_to, 0] = real[part_of]
                send_b[a, slab_to, 1] = imag[part_of]
                source = send_b.at[a, slab_to]
                target = got_b.at[a, :, pl.ds(0, KROWS), lane_slab(slab)]

                @pl.when(slab_to == slab)
                def _():
                    pltpu.make_async_copy(source, target, recv_sem.at[1, a]).start()

                @pl.when(slab_to != slab)
                def _():
                    pltpu.make_async_remote_copy(
                        src_ref=source, dst_ref=target,
                        send_sem=send_sem.at[1, a], recv_sem=recv_sem.at[1, a],
                        device_id=place(z, slab_to), device_id_type=MESH,
                    ).start()

            return carry

        lax.fori_loop(0, SLABS // 2, step, 0)

    first = slab == 0
    top = lax.broadcasted_iota(jnp.int32, (8, SIDE), 0) == 0

    def cols_forward(a):
        arrived = got_b.at[a, :, pl.ds(0, KROWS)]
        pltpu.make_async_copy(arrived, arrived, recv_sem.at[1, a]).wait()
        head = got_b[a, 1, 0:8]
        lone = jnp.broadcast_to(head[0:1], (8, SIDE))
        got_b[a, 0, KROWS:PAD] = -lone * shift_ref[0:1]
        got_b[a, 1, KROWS:PAD] = lone * shift_ref[1:2]
        got_b[a, 1, 0:8] = jnp.where(jnp.logical_and(top, first), 0.0, head)
        real = [got_b[a, 0, :, i * QUARTER : (i + 1) * QUARTER] for i in range(RADIX)]
        imag = [got_b[a, 1, :, i * QUARTER : (i + 1) * QUARTER] for i in range(RADIX)]
        sum_r, dif_r = real[0] + real[2], real[0] - real[2]
        sum_i, dif_i = imag[0] + imag[2], imag[0] - imag[2]
        sum_r2, dif_r2 = real[1] + real[3], real[1] - real[3]
        sum_i2, dif_i2 = imag[1] + imag[3], imag[1] - imag[3]
        mixed = [
            (sum_r + sum_r2, sum_i + sum_i2),
            (dif_r + dif_i2, dif_i - dif_r2),
            (sum_r - sum_r2, sum_i - sum_i2),
            (dif_r - dif_i2, dif_i + dif_r2),
        ]
        lines = []
        for m, (re, im) in enumerate(mixed):
            if m:
                cos, sin = twist_ref[m : m + 1], twist_ref[RADIX + m : RADIX + m + 1]
                re, im = re * cos + im * sin, im * cos - re * sin
            lines.append(jnp.concatenate([re, im], axis=1))
        high, low = split(jnp.concatenate(lines, axis=0))
        spec[a] = dot(high, cols_in[0]) + dot(low, cols_in[0]) + dot(high, cols_in[1])

    def cols_back(a, real, imag):
        high, low = split(jnp.concatenate([real, imag], axis=1))
        back = dot(high, cols_out[0]) + dot(low, cols_out[0]) + dot(high, cols_out[1])
        pieces = []
        for m in range(RADIX):
            re = back[m * PAD : (m + 1) * PAD, :QUARTER]
            im = back[m * PAD : (m + 1) * PAD, QUARTER:]
            if m:
                cos, sin = twist_ref[m : m + 1], twist_ref[RADIX + m : RADIX + m + 1]
                re, im = re * cos - im * sin, im * cos + re * sin
            pieces.append((re, im))
        (r0, i0), (r1, i1), (r2, i2), (r3, i3) = pieces
        sum_r, dif_r, sum_i, dif_i = r0 + r2, r0 - r2, i0 + i2, i0 - i2
        sum_r2, dif_r2, sum_i2, dif_i2 = r1 + r3, r1 - r3, i1 + i3, i1 - i3
        out_r = jnp.concatenate(
            [sum_r + sum_r2, dif_r - dif_i2, sum_r - sum_r2, dif_r + dif_i2], axis=1
        )
        out_i = jnp.concatenate(
            [sum_i + sum_i2, dif_i + dif_r2, sum_i - sum_i2, dif_i - dif_r2], axis=1
        )
        lone = out_i[KROWS : KROWS + 1] * shift_ref[1:2] - out_r[KROWS : KROWS + 1] * shift_ref[0:1]
        send_c[a, 0] = out_r[:KROWS]
        send_c[a, 1] = out_i[:KROWS]
        send_c[a, 1, 0:8] = jnp.where(jnp.logical_and(top, first), lone, out_i[0:8])
        target = got_c.at[a, :, k_rows(slab)]
        pltpu.make_async_copy(
            send_c.at[a, :, :, lane_slab(slab)], target, recv_sem.at[2, a]
        ).start()

        def step(i, carry):
            slab_to = lax.rem(slab + i, SLABS)
            pltpu.make_async_remote_copy(
                src_ref=send_c.at[a, :, :, lane_slab(slab_to)], dst_ref=target,
                send_sem=send_sem.at[2, a], recv_sem=recv_sem.at[2, a],
                device_id=place(z, slab_to), device_id_type=MESH,
            ).start()
            return carry

        lax.fori_loop(1, SLABS, step, 0)

    scale = 2.0 / (SIDE * SIDE * SIDE)

    def rows_back(a):
        pltpu.make_async_copy(got_c.at[a], got_c.at[a], recv_sem.at[2, a]).wait()
        real, imag = got_c[a, 0], got_c[a, 1]
        cos, sin = turn[0], turn[1]
        high, low = split(real * cos - imag * sin)
        halves[:HALF, :LANES] = high
        halves[:HALF, LANES:] = low
        high, low = split(imag * cos + real * sin)
        halves[HALF:, :LANES] = high
        halves[HALF:, LANES:] = low

        def step(i, carry):
            at = pl.ds(pl.multiple_of(i * 256, 256), 256)
            wide = dot(rows_out[0, at], halves[...])
            both = wide[:, :LANES] + wide[:, LANES:] + dot(rows_out[1, at], halves[:, :LANES])
            done[a, at] = both * scale
            return carry

        lax.fori_loop(0, SIDE // 256, step, 0)
        target = got_d.at[a, z, :, lane_slab(slab)]
        pltpu.make_async_copy(done.at[a, row_block(block)], target, recv_sem.at[3, a]).start()

        def send(i, carry):
            z_to, slab_to = partner(i)
            to = place(z_to, slab_to)
            pltpu.make_async_remote_copy(
                src_ref=done.at[a, row_block(to["row"] * lax.axis_size("col") + to["col"])],
                dst_ref=target,
                send_sem=send_sem.at[3, a], recv_sem=recv_sem.at[3, a],
                device_id=to, device_id_type=MESH,
            ).start()
            return carry

        lax.fori_loop(1, ZS * SLABS, send, 0)

    def halves_of(a):
        return spec[a, :, :QUARTER], spec[a, :, QUARTER:]

    consts[0].wait()
    consts[1].wait()
    rows_forward(0)
    rows_forward(1)
    consts[2].wait()
    cols_forward(0)
    cols_forward(1)
    consts[3].wait()
    hr, hi = halves_of(0)
    gr, gi = halves_of(1)
    cols_back(0, hr * gr - hi * gi, hr * gi + hi * gr)
    rows_forward(2)
    consts[4].wait()
    rows_back(0)
    cols_forward(2)
    hr, hi = halves_of(0)
    cr, ci = halves_of(2)
    cols_back(1, hr * cr + hi * ci, hr * ci - hi * cr)
    gr, gi = halves_of(1)
    cols_back(2, gr * cr + gi * ci, gr * ci - gi * cr)
    rows_back(1)
    rows_back(2)

    pltpu.make_async_copy(got_d.at[0], got_d.at[0], recv_sem.at[3, 0]).wait()
    d_outer_ref[...] = (grad_ref[...].astype(F32) * got_d[0]).astype(BF16)
    pltpu.make_async_copy(got_d.at[1], got_d.at[1], recv_sem.at[3, 1]).wait()
    d_inner_ref[...] = (got_d[1] * signal_ref[...].astype(F32)).astype(BF16)
    d_signal_ref[...] = (got_d[1] * inner_ref[...].astype(F32)).astype(BF16)
    pltpu.make_async_copy(got_d.at[2], got_d.at[2], recv_sem.at[3, 2]).wait()
    part[...] = jnp.sum(got_d[2], axis=0)
    for i in range(1, dps):
        pltpu.make_async_remote_copy(
            src_ref=part, dst_ref=got_e.at[i - 1],
            send_sem=send_sem.at[4, 0], recv_sem=recv_sem.at[4, 0],
            device_id={"dp": lax.rem(x + i, dps)}, device_id_type=MESH,
        ).start()
    pltpu.make_async_copy(got_e, got_e, recv_sem.at[4, 0]).wait()
    d_taps_ref[...] = part[...] + got_e[0] + got_e[1] + got_e[2]

    for a in range(ARRAYS):
        sent = [
            got_a.at[a, pl.ds(0, SIDE - ROWS)],
            got_b.at[a, :, pl.ds(0, KROWS), pl.ds(0, SIDE - LANES)],
            got_c.at[a, :, pl.ds(0, HALF - KROWS)],
            done.at[a, pl.ds(0, SIDE - ROWS)],
        ]
        for phase, ref in enumerate(sent):
            pltpu.make_async_copy(ref, ref, send_sem.at[phase, a]).wait()
    pltpu.make_async_copy(got_e, got_e, send_sem.at[4, 0]).wait()


def shards(consts, outer_gate, inner_gate, signal, grad_out, filter_weight):
    rows_in, rows_out, cols_in, cols_out, turn, twist, shift = consts
    shape = outer_gate.shape[1:]
    vmem = pl.BlockSpec(memory_space=pltpu.VMEM)
    anywhere = pl.BlockSpec(memory_space=pl.ANY)
    outs = pl.pallas_call(
        kernel,
        out_shape=[jax.ShapeDtypeStruct(shape, BF16)] * 3
        + [jax.ShapeDtypeStruct(filter_weight.shape, F32)],
        in_specs=[vmem] * 7 + [anywhere] * 5,
        out_specs=[vmem] * 4,
        scratch_shapes=[
            pltpu.VMEM(rows_in.shape, BF16),
            pltpu.VMEM(rows_out.shape, BF16),
            pltpu.VMEM(cols_in.shape, BF16),
            pltpu.VMEM(cols_out.shape, BF16),
            pltpu.VMEM((2, HALF, LANES), F32),
            pltpu.VMEM(shape, F32),
            pltpu.VMEM(shape, F32),
            pltpu.VMEM((ARRAYS, SIDE, LANES), F32),
            pltpu.VMEM((ARRAYS, SLABS, 2, KROWS, LANES), F32),
            pltpu.VMEM((ARRAYS, 2, PAD, SIDE), F32),
            pltpu.VMEM((ARRAYS, RADIX * PAD, 2 * QUARTER), F32),
            pltpu.VMEM((ARRAYS, 2, KROWS, SIDE), F32),
            pltpu.VMEM((ARRAYS, 2, HALF, LANES), F32),
            pltpu.VMEM((ARRAYS, SIDE, LANES), F32),
            pltpu.VMEM((ARRAYS, ZS, ROWS, SIDE), F32),
            pltpu.VMEM((ROWS, SIDE), F32),
            pltpu.VMEM((3, ROWS, SIDE), F32),
            pltpu.VMEM((SIDE, 2 * LANES), BF16),
            pltpu.SemaphoreType.DMA((5,)),
            pltpu.SemaphoreType.DMA((5, ARRAYS)),
            pltpu.SemaphoreType.DMA((5, ARRAYS)),
        ],
        compiler_params=pltpu.CompilerParams(
            collective_id=0, has_side_effects=True, vmem_limit_bytes=56 * 1024 * 1024
        ),
    )(
        outer_gate[0], inner_gate[0], signal[0], grad_out[0], filter_weight, twist, shift,
        rows_in, rows_out, cols_in, cols_out, turn,
    )
    return outs[0][None], outs[1][None], outs[2][None], outs[3]


def solution(mesh):
    placed = P("dp", None, ("row", "col"), None)
    grid = P(("row", "col"), None)
    consts = tuple(jnp.asarray(table) for table in tables())
    return jax.shard_map(
        functools.partial(shards, consts),
        mesh=mesh,
        in_specs=(placed, placed, placed, placed, grid),
        out_specs=(placed, placed, placed, grid),
        check_vma=False,
    )
```

time: 540 us -> 123 us (0.23); the launches traced: 530 us -> 123 us
  local copies, waits for them, and re-layouts: 176 us -> 6.48 us
  Pallas kernels: 0 us -> 115 us
  blocking collectives: 113 us -> 0 us
  waiting for transfers between devices: 77.6 us -> 0 us
  matrix products: 70 us -> 0 us
  starting transfers between devices: 39 us -> 0 us
  other arithmetic: 38.2 us -> 0 us
  between operations: 15.3 us -> 0.64 us
    pallas_call x0 -> x1, Pallas kernels: none -> 115 us  [shards(): pl.pallas_call(kernel, out_shape=[jax.ShapeDtypeStruct(shape, BF16)] * 3...]
    all_to_all x2 -> x0, blocking collectives: 113 us -> none  [redistribute(): lax.all_to_all(blocks, ('row', 'col'), split_axis=0, concat_axis=0, tiled...]
    dot_general x42 -> x0, matrix products: 70 us -> none  [contract(): jnp.einsum(form, left, right, precision=lax.Precision.HIGHEST, preferred_...]
    another operation x20 -> x0, local copies, waits for them, and re-layouts: 56.9 us -> none  [the longest x5 13.8 us: axis_dft(): real_three = real.reshape(first, second, width)]
    all_to_all x4 -> x0, waiting for transfers between devices: 54.2 us -> none  [redistribute(): lax.all_to_all(blocks, ('row', 'col'), split_axis=0, concat_axis=0, tiled...]
    all_to_all x4 -> x0, starting transfers between devices: 39 us -> none  [redistribute(): lax.all_to_all(blocks, ('row', 'col'), split_axis=0, concat_axis=0, tiled...]
    reshape x7 -> x0, local copies, waits for them, and re-layouts: 28.8 us -> none  [the longest x4 20.8 us: forward(): jnp.concatenate([turned_real, turned_imag], axis=1)]
    transpose x7 -> x0, local copies, waits for them, and re-layouts: 23.9 us -> none  [the longest x4 12.6 us: forward(): jnp.transpose(gotten[:, :, count:, :], (0, 3, 1, 2))]
  transfers between devices with their start and end apart: 5 -> 0, of which waited for: 3 -> 0; matrix products, arithmetic and copies ran while one was open for 20% -> 0% of each run, Pallas kernels for 0% -> 0%
where the time goes in v1:
time: 123 us
  Pallas kernels  115 us (93%)
  local copies, waits for them, and re-layouts  6.48 us (5%)
    pallas_call x1, Pallas kernels, shards(): pl.pallas_call(kernel, out_shape=[jax.ShapeDtypeStruct(shape, BF16)] * 3...  115 us
    unnamed x4, local copies, waits for them, and re-layouts  6.48 us

profile of v1, /device:TPU:1, one launch (start us, length us, event | category | flops | bytes accessed | tf_op | source)
XLA Modules:
  0.0 122.6 jit_solution(14708236784021530698)
XLA Ops:
  0.6 115.5 %shard_map.147 = (bf16[8,16,1024]{2,1,0:T(8,128)(2,1)}, bf16[8,16,1024]{2,1,0:T(8,128)(2,1)}, bf16[8,16,1024]{2,1,0:T(8,128)(2,1)}, f32[16,1024]{1,0:T(8,128)}) custom-call(bf16[8,16,1024]{2,1,0:T(8,128)(2,1)} %bitcast.7, bf16[8,16,1024]{2,1,0:T(8,128)(2,1)} %bitcast.8, bf16[8,16,1024]{2,1,0:T(8,128)(2,1)} %bitcast.9, bf16[8,16,1024]{2,1,0:T(8,128)(2,1)} %bitcast.10, ...), custom_call_target="tpu_custom_call" | custom-call | tf_op jit(solution)/shard_map/pallas_call | solution.py:372
  116.1 1.7 %copy.20 = bf16[1,8,16,1024]{3,2,1,0:T(8,128)(2,1)} copy(bf16[1,8,16,1024]{3,2,1,0:T(8,128)(2,1)} %bitcast.13) | data formatting | bytes 524288
  117.8 1.7 %copy.21 = bf16[1,8,16,1024]{3,2,1,0:T(8,128)(2,1)} copy(bf16[1,8,16,1024]{3,2,1,0:T(8,128)(2,1)} %bitcast.12) | data formatting | bytes 524288
  119.4 1.7 %copy.22 = bf16[1,8,16,1024]{3,2,1,0:T(8,128)(2,1)} copy(bf16[1,8,16,1024]{3,2,1,0:T(8,128)(2,1)} %bitcast.11) | data formatting | bytes 524288
  121.1 1.5 %copy.23 = f32[16,1024]{1,0:T(8,128)} copy(f32[16,1024]{1,0:T(8,128)} %get-tuple-element.19) | data formatting | bytes 131072

commit v2 on v1

v2 whole, which is shorter than its diff:
```python
import functools
import math

import jax
import jax.numpy as jnp
import ml_dtypes
import numpy as np
from jax import lax
from jax.experimental import pallas as pl
from jax.experimental.pallas import tpu as pltpu
from jax.sharding import PartitionSpec as P

MESH = pl.DeviceIdType.MESH
F32 = jnp.float32
BF16 = jnp.bfloat16

SIDE = 1024
ROWS = 16
ZS = 8
SLABS = 8
CHIPS = 4
DPS = 4
LINES = SIDE // ZS
KROWS = LINES // 2
PIECE = KROWS // DPS
LANES = 128
RADIX = 4
QUARTER = SIDE // RADIX
CHUNKS = 4
WIDTH = SIDE // CHUNKS
EXTRA = 16
ROOT = math.sqrt(0.5)
SCALE = 2.0 / SIDE**3


def split_np(matrix):
    high = matrix.astype(np.float32).astype(ml_dtypes.bfloat16)
    low = (matrix - high.astype(np.float64)).astype(np.float32).astype(ml_dtypes.bfloat16)
    return np.stack([high, low])


def tables():
    step = np.arange(KROWS)
    lists = [np.concatenate([8 * step, 8 * step + 4])]
    lists += [8 * np.arange(LINES) + y for y in range(1, CHIPS)]
    line = np.arange(LINES)
    rows_in, rows_out, turn = [], [], []
    side = np.arange(SIDE)
    for y, k1 in enumerate(lists):
        angle = 2 * np.pi * ((k1[:, None] * line[None, :]) % SIDE) / SIDE
        cos, sin = np.cos(angle), np.sin(angle)
        weight = np.ones(2 * LINES)
        if y == 0:
            none = np.zeros((KROWS, LINES))
            sin[0] = (-1.0) ** line
            matrix = np.block(
                [[cos[:KROWS], none], [none, cos[KROWS:]], [-sin[:KROWS], none], [none, -sin[KROWS:]]]
            )
            weight[0] = weight[LINES] = 0.5
        else:
            matrix = np.block([[cos, sin], [-sin, cos]])
        rows_in.append(split_np(matrix))
        rows_out.append(split_np((matrix * weight[:, None]).T * SCALE))
        angle = 2 * np.pi * ((k1[:, None] * side[None, :]) % SIDE**2) / SIDE**2
        turn.append(np.stack([np.cos(angle), np.sin(angle)]).astype(np.float32))
    quarter = np.arange(QUARTER)
    small = 2 * np.pi * ((quarter[:, None] * quarter[None, :]) % QUARTER) / QUARTER
    cos, sin = np.cos(small), np.sin(small)
    cols_in = split_np(np.block([[cos, -sin], [sin, cos]]))
    cols_out = split_np(np.block([[cos, sin], [-sin, cos]]))
    twist = 2 * np.pi * np.arange(RADIX)[:, None] * quarter[None, :] / SIDE
    twist = np.concatenate([np.cos(twist), np.sin(twist)], axis=0).astype(np.float32)
    shift = np.pi * side / SIDE
    shift = np.stack([np.cos(shift), np.sin(shift)] * 4).astype(np.float32)
    return np.stack(rows_in), np.stack(rows_out), cols_in, cols_out, np.stack(turn), twist, shift


def split(value):
    high = value.astype(BF16)
    return high, (value - high.astype(F32)).astype(BF16)


def dot(left, right):
    return jnp.dot(left, right, preferred_element_type=F32)


def blocks_forward(x):
    e0, e1, e2, e3 = x[0] + x[4], x[1] + x[5], x[2] + x[6], x[3] + x[7]
    d0, d1, d2, d3 = x[0] - x[4], x[1] - x[5], x[2] - x[6], x[3] - x[7]
    even, odd = e0 + e2, e1 + e3
    less, more = ROOT * (d1 - d3), ROOT * (d1 + d3)
    return (
        even + odd, even - odd,
        d0 + less, -d2 - more,
        e0 - e2, e3 - e1,
        d0 - less, d2 - more,
    )


def blocks_back(u):
    u0, u4, a, b, c, d, e, f = u
    plus, minus = u0 + u4, u0 - u4
    even = (plus + c, minus - d, plus - c, minus + d)
    less, more = ROOT * (a - e), ROOT * (b + f)
    odd = (a + e, less - more, f - b, -less - more)
    return [even[i] + odd[i] for i in range(4)] + [even[i] - odd[i] for i in range(4)]


def kernel(
    outer_ref, inner_ref, signal_ref, grad_ref, taps_ref, twist_ref, shift_ref,
    rows_in_hbm, rows_out_hbm, cols_in_hbm, cols_out_hbm, turn_hbm,
    conv_ref, back_ref, d_taps_ref,
    rows_in, rows_out, cols_in, cols_out, turn, turn_f,
    gated, got_a, send_b, got_b, send_q, got_q, spec, spec_x, send_r, got_r, send_c, got_c, done, got_d,
    f1, f2s, f2, f3s, f3, f4s, f4xs, f4x, t4s, t4, t4xs, t4x, t3s, t3, t5s, t5, t2s, t2, t1s, t1,
    const_sem, send_sem, recv_sem,
):
    x = lax.axis_index("dp")
    row = lax.axis_index("row")
    col = lax.axis_index("col")
    slab = lax.rem(col, SLABS)
    zpos = (col // SLABS) * 4 + row
    zid = row * 2 + col // SLABS
    y = slab // 2
    core = lax.rem(slab, 2)
    mate = 1 - core

    def at_z(i):
        other = lax.rem(zpos + i, ZS)
        row_to, high = lax.rem(other, 4), other // 4
        return row_to * 2 + high, {"row": row_to, "col": high * SLABS + slab}

    def at_slab(slab_to):
        return {"col": (col // SLABS) * SLABS + slab_to}

    def wide(k):
        return pl.ds(pl.multiple_of(k * WIDTH, WIDTH), WIDTH)

    def lanes(k):
        return pl.ds(pl.multiple_of(k * LANES, LANES), LANES)

    def rows(k, count):
        return pl.ds(pl.multiple_of(k * count, count), count)

    consts = [
        pltpu.make_async_copy(source, target, const_sem.at[i])
        for i, (source, target) in enumerate(
            [
                (rows_in_hbm.at[y], rows_in),
                (turn_hbm.at[y, :, :, lanes(zid)], turn_f),
                (turn_hbm.at[y, :, :, wide(core)], turn.at[0]),
                (turn_hbm.at[y, :, :, wide(core + 2)], turn.at[1]),
                (cols_in_hbm, cols_in),
                (cols_out_hbm, cols_out),
                (rows_out_hbm.at[y], rows_out),
            ]
        )
    ]
    for copy in consts:
        copy.start()

    barrier = pltpu.get_barrier_semaphore()
    order = (4, 3, 5, 2, 6, 1, 7)
    partners = [at_z(i)[1] for i in order]
    partners += [at_slab(lax.rem(slab + i, SLABS)) for i in range(1, SLABS)]
    for i in range(1, DPS):
        to = lax.rem(x + i, DPS)
        partners += [{"dp": to}, {"dp": to, **at_slab(slab + 1 - 2 * core)}]
    for device in partners:
        pl.semaphore_signal(barrier, inc=1, device_id=device, device_id_type=MESH)
    gated[0] = inner_ref[...].astype(F32) * signal_ref[...].astype(F32)
    gated[1] = grad_ref[...].astype(F32) * outer_ref[...].astype(F32)
    pl.semaphore_wait(barrier, len(partners))

    names = {}

    def sem(name):
        return names.setdefault(name, len(names))

    for name in ["a", "c", "d"]:
        for k in range(2 * CHUNKS):
            sem((name, k))
    for name in ["b", "r"]:
        for k in range(4):
            sem((name, k))
    pending = []

    def push(source, target, index, device):
        pltpu.make_async_remote_copy(
            src_ref=source, dst_ref=target,
            send_sem=send_sem.at[index], recv_sem=recv_sem.at[index],
            device_id=device, device_id_type=MESH,
        ).start()

    def keep(source, target, index):
        pltpu.make_async_copy(source, target, recv_sem.at[index]).start()

    def await_all(ref, index):
        pltpu.make_async_copy(ref, ref, recv_sem.at[index]).wait()

    def sent(ref, index):
        pending.append((ref, index))

    def over_z(name, source_of, target):
        index = sem(name)
        keep(source_of(zid), target, index)
        for i in order:
            z_to, device = at_z(i)
            push(source_of(z_to), target, index, device)
        return index

    def send_a(a, k):
        at = pl.ds(k * WIDTH, WIDTH)
        index = over_z(
            ("a", a * CHUNKS + k), lambda z_to: gated.at[a, z_to, :, at], got_a.at[a, zid, :, at]
        )
        sent(got_a.at[a, pl.ds(0, ZS - 1), :, at], index)

    def send_bs(a, k):
        at = pl.ds(k * WIDTH, WIDTH)
        index = sem(("a", a * CHUNKS + k))
        await_all(got_a.at[a, :, :, at], index)
        units = blocks_forward([got_a[a, i, :, k * WIDTH : (k + 1) * WIDTH] for i in range(ZS)])
        for u, value in enumerate(units):
            send_b[a, u, :, k * WIDTH : (k + 1) * WIDTH] = value
        core_to, i = k % 2, k // 2
        index = sem(("b", a * 2 + i))
        target = got_b.at[a, i, :, rows(slab, ROWS)]
        for dy in range(CHIPS):
            y_to = lax.rem(y + dy, CHIPS)
            source = send_b.at[a, pl.ds(y_to * 2, 2), :, at]
            device = at_slab(y_to * 2 + core_to)
            if dy:
                push(source, target, index, device)
            else:
                @pl.when(core == core_to)
                def _():
                    keep(source, target, index)

                @pl.when(core != core_to)
                def _():
                    push(source, target, index, device)

    def rows_forward(a, i):
        await_all(got_b.at[a, i], sem(("b", a * 2 + i)))
        high, low = split(jnp.concatenate([got_b[a, i, 0], got_b[a, i, 1]], axis=0))
        both = dot(rows_in[0], high) + dot(rows_in[0], low) + dot(rows_in[1], high)
        re, im = both[:LINES], both[LINES:]
        cos, sin = turn[i, 0], turn[i, 1]
        send_q[a, i, 0] = re * cos + im * sin
        send_q[a, i, 1] = im * cos - re * sin
        index = sem(("q", a))
        target = got_q.at[a, :, :, wide(core + 2 * i)]
        keep(send_q.at[a, i, :, rows(core, KROWS)], target, index)
        push(send_q.at[a, i, :, rows(mate, KROWS)], target, index, at_slab(y * 2 + mate))

    first = slab == 0
    top = lax.broadcasted_iota(jnp.int32, (8, SIDE), 0) == 0
    line_8 = lax.broadcasted_iota(jnp.int32, (8, 2 * QUARTER), 0)

    def radix_in(real, imag):
        r = [real[:, i * QUARTER : (i + 1) * QUARTER] for i in range(RADIX)]
        m = [imag[:, i * QUARTER : (i + 1) * QUARTER] for i in range(RADIX)]
        sum_r, dif_r, sum_i, dif_i = r[0] + r[2], r[0] - r[2], m[0] + m[2], m[0] - m[2]
        sum_r2, dif_r2, sum_i2, dif_i2 = r[1] + r[3], r[1] - r[3], m[1] + m[3], m[1] - m[3]
        mixed = [
            (sum_r + sum_r2, sum_i + sum_i2),
            (dif_r + dif_i2, dif_i - dif_r2),
            (sum_r - sum_r2, sum_i - sum_i2),
            (dif_r - dif_i2, dif_i + dif_r2),
        ]
        parts = []
        for m, (re, im) in enumerate(mixed):
            if m:
                cos, sin = twist_ref[m : m + 1], twist_ref[RADIX + m : RADIX + m + 1]
                re, im = re * cos + im * sin, im * cos - re * sin
            parts.append(jnp.concatenate([re, im], axis=1))
        return parts

    def radix_out(parts):
        pieces = []
        for m, part in enumerate(parts):
            re, im = part[:, :QUARTER], part[:, QUARTER:]
            if m:
                cos, sin = twist_ref[m : m + 1], twist_ref[RADIX + m : RADIX + m + 1]
                re, im = re * cos - im * sin, im * cos + re * sin
            pieces.append((re, im))
        (r0, i0), (r1, i1), (r2, i2), (r3, i3) = pieces
        sum_r, dif_r, sum_i, dif_i = r0 + r2, r0 - r2, i0 + i2, i0 - i2
        sum_r2, dif_r2, sum_i2, dif_i2 = r1 + r3, r1 - r3, i1 + i3, i1 - i3
        out_r = jnp.concatenate(
            [sum_r + sum_r2, dif_r - dif_i2, sum_r - sum_r2, dif_r + dif_i2], axis=1
        )
        out_i = jnp.concatenate(
            [sum_i + sum_i2, dif_i + dif_r2, sum_i - sum_i2, dif_i - dif_r2], axis=1
        )
        return out_r, out_i

    def cols_forward(real, imag, special):
        head = imag[0:8]
        lone = head[0:1]
        extra = radix_in(-lone * shift_ref[0:1], lone * shift_ref[1:2])
        tail = jnp.zeros((8, 2 * QUARTER), F32)
        for m in range(RADIX):
            tail = jnp.where(line_8 == m, extra[m], tail)
        head = jnp.where(jnp.logical_and(top, special), 0.0, head)
        imag = jnp.concatenate([head, imag[8:]], axis=0)
        high, low = split(jnp.concatenate(radix_in(real, imag) + [tail, tail], axis=0))
        return dot(high, cols_in[0]) + dot(low, cols_in[0]) + dot(high, cols_in[1])

    def cols_back(parts, extra, special):
        count = parts.shape[1]
        stacked = jnp.concatenate([parts[m] for m in range(RADIX)] + [extra, extra], axis=0)
        high, low = split(stacked)
        back = dot(high, cols_out[0]) + dot(low, cols_out[0]) + dot(high, cols_out[1])
        tail = back[RADIX * count : RADIX * count + 8]
        lone_r, lone_i = radix_out([tail[m : m + 1] for m in range(RADIX)])
        lone = lone_i * shift_ref[1:2] - lone_r * shift_ref[0:1]
        out_r, out_i = radix_out([back[m * count : (m + 1) * count] for m in range(RADIX)])
        head = jnp.where(jnp.logical_and(top, special), lone, out_i[0:8])
        return out_r, jnp.concatenate([head, out_i[8:]], axis=0)

    def spectrum(a):
        await_all(got_q.at[a], sem(("q", a)))
        sent(send_q.at[a, :, :, pl.ds(0, KROWS)], sem(("q", a)))
        both = cols_forward(got_q[a, 0], got_q[a, 1], first)
        for m in range(RADIX):
            spec[a + 1, m] = both[m * KROWS : (m + 1) * KROWS]
        spec_x[a + 1] = both[RADIX * KROWS : RADIX * KROWS + 8]

    def times(left, right):
        lr, li = left[..., :QUARTER], left[..., QUARTER:]
        rr, ri = right[..., :QUARTER], right[..., QUARTER:]
        return jnp.concatenate([lr * rr - li * ri, lr * ri + li * rr], axis=-1)

    def conj_times(left, right):
        lr, li = left[..., :QUARTER], left[..., QUARTER:]
        rr, ri = right[..., :QUARTER], right[..., QUARTER:]
        return jnp.concatenate([lr * rr + li * ri, lr * ri - li * rr], axis=-1)

    def send_rs(a, parts, extra):
        out_r, out_i = cols_back(parts, extra, first)
        send_r[a, 0] = out_r
        send_r[a, 1] = out_i
        for i in range(2):
            index = sem(("r", a * 2 + i))
            target = got_r.at[a, i, :, rows(core, KROWS)]
            keep(send_r.at[a, :, :, wide(core + 2 * i)], target, index)
            push(send_r.at[a, :, :, wide(mate + 2 * i)], target, index, at_slab(y * 2 + mate))
            sent(got_r.at[a, i, :, pl.ds(0, KROWS)], index)

    def rows_back(a, i):
        await_all(got_r.at[a, i], sem(("r", a * 2 + i)))
        real, imag = got_r[a, i, 0], got_r[a, i, 1]
        cos, sin = turn[i, 0], turn[i, 1]
        high, low = split(
            jnp.concatenate([real * cos - imag * sin, imag * cos + real * sin], axis=0)
        )
        both = dot(rows_out[0], high) + dot(rows_out[0], low) + dot(rows_out[1], high)
        send_c[a, i, 0] = both[:LINES]
        send_c[a, i, 1] = both[LINES:]
        base = sem(("c", a * CHUNKS))
        k = core + 2 * i
        target = got_c.at[a, pl.ds(y * 2, 2), :, wide(k)]
        keep(send_c.at[a, i, :, rows(slab, ROWS)], target, base + k)
        for j in range(1, SLABS):
            slab_to = lax.rem(slab + j, SLABS)
            push(send_c.at[a, i, :, rows(slab_to, ROWS)], target, base + k, at_slab(slab_to))
        sent(send_c.at[a, i, :, pl.ds(0, (SLABS - 1) * ROWS)], base + k)

    def send_ds(a, k):
        at = pl.ds(k * WIDTH, WIDTH)
        await_all(got_c.at[a, :, :, at], sem(("c", a * CHUNKS + k)))
        out = blocks_back([got_c[a, u, :, k * WIDTH : (k + 1) * WIDTH] for u in range(8)])
        for i, value in enumerate(out):
            done[a, i, :, k * WIDTH : (k + 1) * WIDTH] = value
        index = over_z(
            ("d", a * CHUNKS + k), lambda z_to: done.at[a, z_to, :, at], got_d.at[a, zid, :, at]
        )
        sent(got_d.at[a, pl.ds(0, ZS - 1), :, at], index)

    index = over_z("f1", lambda z_to: taps_ref.at[:, lanes(z_to)], f1.at[zid])
    sent(f1.at[pl.ds(0, ZS - 1)], index)
    for k in range(3):
        send_a(0, k)

    await_all(f1, sem("f1"))
    for u, value in enumerate(blocks_forward([f1[i] for i in range(ZS)])):
        f2s[u] = value
    index = sem("f2")
    target = f2.at[:, rows(slab, ROWS)]
    keep(f2s.at[pl.ds(y * 2, 2)], target, index)
    for j in range(1, SLABS):
        slab_to = lax.rem(slab + j, SLABS)
        push(f2s.at[pl.ds((slab_to // 2) * 2, 2)], target, index, at_slab(slab_to))
    sent(f2.at[:, pl.ds(0, (SLABS - 1) * ROWS)], index)

    send_bs(0, 0)
    consts[0].wait()
    consts[1].wait()
    await_all(f2, sem("f2"))
    high, low = split(jnp.concatenate([f2[0], f2[1]], axis=0))
    mine = core * (KROWS // PIECE) + x
    halves = []
    for part in range(2):
        at = pl.ds(pl.multiple_of(part * LINES + mine * PIECE, PIECE), PIECE)
        halves.append(dot(rows_in[0, at], high) + dot(rows_in[0, at], low) + dot(rows_in[1, at], high))
    re, im = halves
    cos, sin = turn_f[0, rows(mine, PIECE)], turn_f[1, rows(mine, PIECE)]
    f3s[0] = re * cos + im * sin
    f3s[1] = im * cos - re * sin
    index = over_z("f3", lambda z_to: f3s, f3.at[:, :, lanes(zid)])
    sent(f3.at[:, :, pl.ds(0, SIDE - LANES)], index)

    send_a(0, 3)
    for k in range(CHUNKS):
        send_a(1, k)
    send_bs(0, 1)
    send_bs(0, 2)

    consts[4].wait()
    await_all(f3, sem("f3"))
    special = jnp.logical_and(first, x == 0)
    both = cols_forward(f3[0], f3[1], special)
    for m in range(RADIX):
        f4s[m] = both[m * PIECE : (m + 1) * PIECE]
    f4xs[...] = both[RADIX * PIECE : RADIX * PIECE + 8]
    index, index_x = sem("f4"), sem("f4x")
    target, target_x = spec.at[0, :, rows(x, PIECE)], f4x.at[x]
    keep(f4s, target, index)
    keep(f4xs, target_x, index_x)
    for i in (2, 1, 3):
        device = {"dp": lax.rem(x + i, DPS)}
        push(f4s, target, index, device)
        push(f4xs, target_x, index_x, device)
    sent(spec.at[0, :, pl.ds(0, (DPS - 1) * PIECE)], index)
    sent(f4x.at[pl.ds(0, DPS - 1)], index_x)

    consts[2].wait()
    consts[3].wait()
    send_bs(0, 3)
    rows_forward(0, 0)
    send_bs(1, 0)
    rows_forward(0, 1)
    spectrum(0)
    send_bs(1, 1)
    consts[5].wait()
    await_all(spec.at[0], sem("f4"))
    await_all(f4x, sem("f4x"))
    spec_x[0] = f4x[0]
    send_rs(0, times(spec[0], spec[1]), times(spec_x[0], spec_x[1]))
    send_bs(1, 2)
    consts[6].wait()
    rows_back(0, 0)
    rows_back(0, 1)
    rows_forward(1, 0)
    send_bs(1, 3)
    send_ds(0, 0)
    send_ds(0, 1)
    rows_forward(1, 1)
    send_ds(0, 2)
    send_ds(0, 3)
    spectrum(1)

    t4s[...] = conj_times(spec[1], spec[2])
    t4xs[...] = conj_times(spec_x[1], spec_x[2])
    index, index_x = sem("t4"), sem("t4x")
    keep(t4s.at[:, rows(x, PIECE)], t4.at[x], index)
    keep(t4xs, t4x.at[x], index_x)
    for i in (2, 1, 3):
        to = lax.rem(x + i, DPS)
        push(t4s.at[:, rows(to, PIECE)], t4.at[x], index, {"dp": to})
        push(t4xs, t4x.at[x], index_x, {"dp": to})
    sent(t4.at[pl.ds(0, DPS - 1)], index)
    sent(t4x.at[pl.ds(0, DPS - 1)], index_x)

    send_rs(1, conj_times(spec[0], spec[2]), conj_times(spec_x[0], spec_x[2]))
    rows_back(1, 0)
    rows_back(1, 1)

    await_all(t4, sem("t4"))
    await_all(t4x, sem("t4x"))
    out_r, out_i = cols_back(
        t4[0] + t4[1] + t4[2] + t4[3], t4x[0] + t4x[1] + t4x[2] + t4x[3], special
    )
    t3s[0] = out_r
    t3s[1] = out_i
    index = over_z("t3", lambda z_to: t3s.at[:, :, lanes(z_to)], t3.at[zid])
    sent(t3.at[pl.ds(0, ZS - 1)], index)
    send_ds(1, 0)
    send_ds(1, 1)

    await_all(t3, sem("t3"))
    t5s[...] = jnp.sum(t3[...], axis=0)
    index = sem("t5")
    target = t5.at[:, rows(mine, PIECE)]
    keep(t5s, target, index)
    push(t5s, target, index, at_slab(y * 2 + mate))
    for i in (2, 1, 3):
        to = lax.rem(x + i, DPS)
        push(t5s, target, index, {"dp": to})
        push(t5s, target, index, {"dp": to, **at_slab(y * 2 + mate)})
    sent(t5.at[:, pl.ds(0, LINES - PIECE)], index)
    send_ds(1, 2)
    send_ds(1, 3)

    await_all(t5, sem("t5"))
    real, imag = t5[0], t5[1]
    cos, sin = turn_f[0], turn_f[1]
    high, low = split(jnp.concatenate([real * cos - imag * sin, imag * cos + real * sin], axis=0))
    both = dot(rows_out[0], high) + dot(rows_out[0], low) + dot(rows_out[1], high)
    t2s[0] = both[:LINES]
    t2s[1] = both[LINES:]
    index = sem("t2")
    target = t2.at[pl.ds(y * 2, 2)]
    keep(t2s.at[:, rows(slab, ROWS)], target, index)
    for dy in (2, 1, 3):
        slab_to = lax.rem(y + dy, CHIPS) * 2 + core
        push(t2s.at[:, rows(slab_to, ROWS)], target, index, at_slab(slab_to))
    sent(t2.at[pl.ds(0, 2 * (CHIPS - 1))], index)

    await_all(t2, sem("t2"))
    for i, value in enumerate(blocks_back([t2[u] for u in range(8)])):
        t1s[i] = value
    index = over_z("t1", lambda z_to: t1s.at[z_to], t1.at[:, lanes(zid)])
    sent(t1.at[:, pl.ds(0, SIDE - LANES)], index)

    for a, ref in enumerate([conv_ref, back_ref]):
        for k in range(CHUNKS):
            await_all(got_d.at[a, :, :, pl.ds(k * WIDTH, WIDTH)], sem(("d", a * CHUNKS + k)))
        ref[...] = got_d[a]
    await_all(t1, sem("t1"))
    d_taps_ref[...] = t1[...]

    for ref, index in pending:
        pltpu.make_async_copy(ref, ref, send_sem.at[index]).wait()
    for a in range(2):
        for i in range(2):
            ref = got_b.at[a, i, :, pl.ds(0, (SLABS - 1) * ROWS)]
            pltpu.make_async_copy(ref, ref, send_sem.at[sem(("b", a * 2 + i))]).wait()


def finish(conv_ref, back_ref, taps_in, grad_ref, signal_ref, inner_ref, outer_out, inner_out, signal_out, taps_out):
    outer_out[...] = (grad_ref[...].astype(F32) * conv_ref[...]).astype(BF16)
    inner_out[...] = (back_ref[...] * signal_ref[...].astype(F32)).astype(BF16)
    signal_out[...] = (back_ref[...] * inner_ref[...].astype(F32)).astype(BF16)
    taps_out[...] = taps_in[...]


def shards(consts, outer_gate, inner_gate, signal, grad_out, filter_weight):
    rows_in, rows_out, cols_in, cols_out, turn, twist, shift = consts
    shape = outer_gate.shape[1:]
    vmem = pl.BlockSpec(memory_space=pltpu.VMEM)
    anywhere = pl.BlockSpec(memory_space=pl.ANY)
    floats = [
        (2, LINES, LANES),
        (2, ZS, ROWS, SIDE),
        (2, ZS, ROWS, SIDE),
        (2, 8, ROWS, SIDE),
        (2, 2, 2, LINES, WIDTH),
        (2, 2, 2, LINES, WIDTH),
        (2, 2, KROWS, SIDE),
        (3, RADIX, KROWS, 2 * QUARTER),
        (3, 8, 2 * QUARTER),
        (2, 2, KROWS, SIDE),
        (2, 2, 2, LINES, WIDTH),
        (2, 2, 2, LINES, WIDTH),
        (2, 8, ROWS, SIDE),
        (2, ZS, ROWS, SIDE),
        (2, ZS, ROWS, SIDE),
        (ZS, ROWS, LANES),
        (8, ROWS, LANES),
        (2, LINES, LANES),
        (2, PIECE, LANES),
        (2, PIECE, SIDE),
        (RADIX, PIECE, 2 * QUARTER),
        (8, 2 * QUARTER),
        (DPS, 8, 2 * QUARTER),
        (RADIX, KROWS, 2 * QUARTER),
        (DPS, RADIX, PIECE, 2 * QUARTER),
        (8, 2 * QUARTER),
        (DPS, 8, 2 * QUARTER),
        (2, PIECE, SIDE),
        (ZS, 2, PIECE, LANES),
        (2, PIECE, LANES),
        (2, LINES, LANES),
        (2, LINES, LANES),
        (8, ROWS, LANES),
        (ZS, ROWS, LANES),
        (ROWS, SIDE),
    ]
    conv, back, d_taps = pl.pallas_call(
        kernel,
        out_shape=[
            jax.ShapeDtypeStruct(shape, F32),
            jax.ShapeDtypeStruct(shape, F32),
            jax.ShapeDtypeStruct(filter_weight.shape, F32),
        ],
        in_specs=[vmem] * 7 + [anywhere] * 5,
        out_specs=[vmem] * 3,
        scratch_shapes=[
            pltpu.VMEM(rows_in.shape[1:], BF16),
            pltpu.VMEM(rows_out.shape[1:], BF16),
            pltpu.VMEM(cols_in.shape, BF16),
            pltpu.VMEM(cols_out.shape, BF16),
            pltpu.VMEM((2, 2, LINES, WIDTH), F32),
        ]
        + [pltpu.VMEM(size, F32) for size in floats]
        + [
            pltpu.SemaphoreType.DMA((7,)),
            pltpu.SemaphoreType.DMA((56,)),
            pltpu.SemaphoreType.DMA((56,)),
        ],
        compiler_params=pltpu.CompilerParams(
            collective_id=0, has_side_effects=True, vmem_limit_bytes=56 * 1024 * 1024
        ),
    )(
        outer_gate[0], inner_gate[0], signal[0], grad_out[0], filter_weight, twist, shift,
        rows_in, rows_out, cols_in, cols_out, turn,
    )
    outs = pl.pallas_call(
        finish,
        out_shape=[jax.ShapeDtypeStruct(shape, BF16)] * 3
        + [jax.ShapeDtypeStruct(filter_weight.shape, F32)],
        in_specs=[vmem] * 6,
        out_specs=[vmem] * 4,
    )(conv, back, d_taps, grad_out[0], signal[0], inner_gate[0])
    return outs[0][None], outs[1][None], outs[2][None], outs[3]


def solution(mesh):
    placed = P("dp", None, ("row", "col"), None)
    grid = P(("row", "col"), None)
    consts = tuple(jnp.asarray(table) for table in tables())
    return jax.shard_map(
        functools.partial(shards, consts),
        mesh=mesh,
        in_specs=(placed, placed, placed, placed, grid),
        out_specs=(placed, placed, placed, grid),
        check_vma=False,
    )
```

time: 123 us -> 82.2 us (0.67)
  Pallas kernels: 115 us -> 81.4 us
  local copies, waits for them, and re-layouts: 6.48 us -> 0 us
    pallas_call x1 -> x2, Pallas kernels: 115 us -> 81.4 us  [the longest x1 79 us: shards(): pl.pallas_call(kernel, out_shape=[jax.ShapeDtypeStruct(shape, F32), jax.S...]
    unnamed x4 -> x0, local copies, waits for them, and re-layouts: 6.48 us -> none
where the time goes in v2:
time: 82.2 us; the launch traced here: 82.1 us
  Pallas kernels  81.4 us (99%)
    pallas_call x1, Pallas kernels, shards(): pl.pallas_call(kernel, out_shape=[jax.ShapeDtypeStruct(shape, F32), jax.S...  79 us
    pallas_call x1, Pallas kernels, shards(): pl.pallas_call(finish, out_shape=[jax.ShapeDtypeStruct(shape, BF16)] * 3...  2.39 us

profile of v2, /device:TPU:1, one launch (start us, length us, event | category | flops | bytes accessed | tf_op | source)
XLA Modules:
  0.0 82.1 jit_solution(5604398266457581849)
XLA Ops:
  0.6 79.0 %shard_map.147 = (f32[8,16,1024]{2,1,0:T(8,128)}, f32[8,16,1024]{2,1,0:T(8,128)}, f32[16,1024]{1,0:T(8,128)}) custom-call(bf16[8,16,1024]{2,1,0:T(8,128)(2,1)} %bitcast.13, bf16[8,16,1024]{2,1,0:T(8,128)(2,1)} %bitcast.7, bf16[8,16,1024]{2,1,0:T(8,128)(2,1)} %bitcast.9, bf16[8,16,1024]{2,1,0:T(8,128)(2,1)} %bitcast.11, f32[16,1024]{1,0:T(8,128)} %taps_ref.1, ...), custom_call_target="tpu_custom_call" | custom-call | tf_op jit(solution)/shard_map/pallas_call | solution.py:592
  79.7 2.4 %shard_map.148 = (bf16[8,16,1024]{2,1,0:T(8,128)(2,1)}, bf16[8,16,1024]{2,1,0:T(8,128)(2,1)}, bf16[8,16,1024]{2,1,0:T(8,128)(2,1)}, f32[16,1024]{1,0:T(8,128)}) custom-call(f32[8,16,1024]{2,1,0:T(8,128)} %get-tuple-element.11.conv_ref, f32[8,16,1024]{2,1,0:T(8,128)} %get-tuple-element.12.back_ref, f32[16,1024]{1,0:T(8,128)} %get-tuple-element.13.taps_in, ...), custom_call_target="tpu_custom_call" | custom-call | tf_op jit(solution)/shard_map/pallas_call | solution.py:621

commit v3 on v2

--- a/solution.py
+++ b/solution.py
@@ -22,13 +22,10 @@
 DPS = 4
 LINES = SIDE // ZS
 KROWS = LINES // 2
-PIECE = KROWS // DPS
-LANES = 128
 RADIX = 4
 QUARTER = SIDE // RADIX
 CHUNKS = 4
 WIDTH = SIDE // CHUNKS
-EXTRA = 16
 ROOT = math.sqrt(0.5)
 SCALE = 2.0 / SIDE**3
 
@@ -107,13 +104,14 @@
 
 
 def kernel(
+    outer_hbm, inner_hbm, signal_hbm, grad_hbm, taps_hbm, twist_hbm, shift_hbm,
+    rows_in_hbm, rows_out_hbm, cols_in_hbm, cols_out_hbm, turn_hbm,
+    d_outer_ref, d_inner_ref, d_signal_ref, d_taps_ref,
     outer_ref, inner_ref, signal_ref, grad_ref, taps_ref, twist_ref, shift_ref,
-    rows_in_hbm, rows_out_hbm, cols_in_hbm, cols_out_hbm, turn_hbm,
-    conv_ref, back_ref, d_taps_ref,
     rows_in, rows_out, cols_in, cols_out, turn, turn_f,
     gated, got_a, send_b, got_b, send_q, got_q, spec, spec_x, send_r, got_r, send_c, got_c, done, got_d,
-    f1, f2s, f2, f3s, f3, f4s, f4xs, f4x, t4s, t4, t4xs, t4x, t3s, t3, t5s, t5, t2s, t2, t1s, t1,
-    const_sem, send_sem, recv_sem,
+    f1, f2s, f2, f3s, t4s, t4, t2s, t2, t1s, t1, t0s, t0,
+    input_sem, const_sem, send_sem, recv_sem,
 ):
     x = lax.axis_index("dp")
     row = lax.axis_index("row")
@@ -136,18 +134,41 @@
     def wide(k):
         return pl.ds(pl.multiple_of(k * WIDTH, WIDTH), WIDTH)
 
-    def lanes(k):
-        return pl.ds(pl.multiple_of(k * LANES, LANES), LANES)
-
     def rows(k, count):
         return pl.ds(pl.multiple_of(k * count, count), count)
 
+    inputs = [
+        pltpu.make_async_copy(source, target, input_sem.at[i])
+        for i, (source, target) in enumerate(
+            [
+                (taps_hbm, taps_ref),
+                (inner_hbm, inner_ref),
+                (signal_hbm, signal_ref),
+                (grad_hbm, grad_ref),
+                (outer_hbm, outer_ref),
+                (twist_hbm, twist_ref),
+                (shift_hbm, shift_ref),
+            ]
+        )
+    ]
+    for copy in inputs:
+        copy.start()
+
+    barrier = pltpu.get_barrier_semaphore()
+    order = (4, 3, 5, 2, 6, 1, 7)
+    partners = [at_z(i)[1] for i in order]
+    partners += [at_slab(lax.rem(slab + i, SLABS)) for i in range(1, SLABS)]
+    for i in range(1, DPS):
+        to = lax.rem(x + i, DPS)
+        partners.append({"dp": to})
+    for device in partners:
+        pl.semaphore_signal(barrier, inc=1, device_id=device, device_id_type=MESH)
     consts = [
         pltpu.make_async_copy(source, target, const_sem.at[i])
         for i, (source, target) in enumerate(
             [
                 (rows_in_hbm.at[y], rows_in),
-                (turn_hbm.at[y, :, :, lanes(zid)], turn_f),
+                (turn_hbm.at[y, :, rows(core, KROWS), wide(x)], turn_f),
                 (turn_hbm.at[y, :, :, wide(core)], turn.at[0]),
                 (turn_hbm.at[y, :, :, wide(core + 2)], turn.at[1]),
                 (cols_in_hbm, cols_in),
@@ -158,16 +179,8 @@
     ]
     for copy in consts:
         copy.start()
-
-    barrier = pltpu.get_barrier_semaphore()
-    order = (4, 3, 5, 2, 6, 1, 7)
-    partners = [at_z(i)[1] for i in order]
-    partners += [at_slab(lax.rem(slab + i, SLABS)) for i in range(1, SLABS)]
-    for i in range(1, DPS):
-        to = lax.rem(x + i, DPS)
-        partners += [{"dp": to}, {"dp": to, **at_slab(slab + 1 - 2 * core)}]
-    for device in partners:
-        pl.semaphore_signal(barrier, inc=1, device_id=device, device_id_type=MESH)
+    for copy in inputs:
+        copy.wait()
     gated[0] = inner_ref[...].astype(F32) * signal_ref[...].astype(F32)
     gated[1] = grad_ref[...].astype(F32) * outer_ref[...].astype(F32)
     pl.semaphore_wait(barrier, len(partners))
@@ -207,6 +220,22 @@
         for i in order:
             z_to, device = at_z(i)
             push(source_of(z_to), target, index, device)
+        return index
+
+    def over_x(name, source_of, target):
+        index = sem(name)
+        keep(source_of(x), target, index)
+        for i in (2, 1, 3):
+            to = lax.rem(x + i, DPS)
+            push(source_of(to), target, index, {"dp": to})
+        return index
+
+    def over_slabs(name, source_of, target):
+        index = sem(name)
+        keep(source_of(slab), target, index)
+        for i in (4, 5, 3, 2, 6, 7, 1):
+            slab_to = lax.rem(slab + i, SLABS)
+            push(source_of(slab_to), target, index, at_slab(slab_to))
         return index
 
     def send_a(a, k):
@@ -249,10 +278,12 @@
         cos, sin = turn[i, 0], turn[i, 1]
         send_q[a, i, 0] = re * cos + im * sin
         send_q[a, i, 1] = im * cos - re * sin
-        index = sem(("q", a))
-        target = got_q.at[a, :, :, wide(core + 2 * i)]
+        index = sem(("q", a + 1))
+        target = got_q.at[a + 1, :, :, wide(core + 2 * i)]
         keep(send_q.at[a, i, :, rows(core, KROWS)], target, index)
         push(send_q.at[a, i, :, rows(mate, KROWS)], target, index, at_slab(y * 2 + mate))
+        if i:
+            sent(send_q.at[a, :, :, pl.ds(0, KROWS)], index)
 
     first = slab == 0
     top = lax.broadcasted_iota(jnp.int32, (8, SIDE), 0) == 0
@@ -322,11 +353,10 @@
 
     def spectrum(a):
         await_all(got_q.at[a], sem(("q", a)))
-        sent(send_q.at[a, :, :, pl.ds(0, KROWS)], sem(("q", a)))
         both = cols_forward(got_q[a, 0], got_q[a, 1], first)
         for m in range(RADIX):
-            spec[a + 1, m] = both[m * KROWS : (m + 1) * KROWS]
-        spec_x[a + 1] = both[RADIX * KROWS : RADIX * KROWS + 8]
+            spec[a, m] = both[m * KROWS : (m + 1) * KROWS]
+        spec_x[a] = both[RADIX * KROWS : RADIX * KROWS + 8]
 
     def times(left, right):
         lr, li = left[..., :QUARTER], left[..., QUARTER:]
@@ -379,158 +409,114 @@
         )
         sent(got_d.at[a, pl.ds(0, ZS - 1), :, at], index)
 
-    index = over_z("f1", lambda z_to: taps_ref.at[:, lanes(z_to)], f1.at[zid])
+    index = over_z("f1", lambda z_to: taps_ref.at[:, wide(x)], f1.at[zid])
     sent(f1.at[pl.ds(0, ZS - 1)], index)
-    for k in range(3):
+    for k in range(CHUNKS):
         send_a(0, k)
 
     await_all(f1, sem("f1"))
     for u, value in enumerate(blocks_forward([f1[i] for i in range(ZS)])):
         f2s[u] = value
-    index = sem("f2")
-    target = f2.at[:, rows(slab, ROWS)]
-    keep(f2s.at[pl.ds(y * 2, 2)], target, index)
-    for j in range(1, SLABS):
-        slab_to = lax.rem(slab + j, SLABS)
-        push(f2s.at[pl.ds((slab_to // 2) * 2, 2)], target, index, at_slab(slab_to))
+    index = over_slabs(
+        "f2", lambda to: f2s.at[pl.ds((to // 2) * 2, 2)], f2.at[:, rows(slab, ROWS)]
+    )
     sent(f2.at[:, pl.ds(0, (SLABS - 1) * ROWS)], index)
 
-    send_bs(0, 0)
     consts[0].wait()
     consts[1].wait()
     await_all(f2, sem("f2"))
     high, low = split(jnp.concatenate([f2[0], f2[1]], axis=0))
-    mine = core * (KROWS // PIECE) + x
     halves = []
     for part in range(2):
-        at = pl.ds(pl.multiple_of(part * LINES + mine * PIECE, PIECE), PIECE)
+        at = pl.ds(pl.multiple_of(part * LINES + core * KROWS, KROWS), KROWS)
         halves.append(dot(rows_in[0, at], high) + dot(rows_in[0, at], low) + dot(rows_in[1, at], high))
     re, im = halves
-    cos, sin = turn_f[0, rows(mine, PIECE)], turn_f[1, rows(mine, PIECE)]
+    cos, sin = turn_f[0], turn_f[1]
     f3s[0] = re * cos + im * sin
     f3s[1] = im * cos - re * sin
-    index = over_z("f3", lambda z_to: f3s, f3.at[:, :, lanes(zid)])
-    sent(f3.at[:, :, pl.ds(0, SIDE - LANES)], index)
-
-    send_a(0, 3)
+    index = over_x(("q", 0), lambda to: f3s, got_q.at[0, :, :, wide(x)])
+    sent(got_q.at[0, :, :, pl.ds(0, SIDE - WIDTH)], index)
+
     for k in range(CHUNKS):
         send_a(1, k)
+    send_bs(0, 0)
     send_bs(0, 1)
     send_bs(0, 2)
-
-    consts[4].wait()
-    await_all(f3, sem("f3"))
-    special = jnp.logical_and(first, x == 0)
-    both = cols_forward(f3[0], f3[1], special)
-    for m in range(RADIX):
-        f4s[m] = both[m * PIECE : (m + 1) * PIECE]
-    f4xs[...] = both[RADIX * PIECE : RADIX * PIECE + 8]
-    index, index_x = sem("f4"), sem("f4x")
-    target, target_x = spec.at[0, :, rows(x, PIECE)], f4x.at[x]
-    keep(f4s, target, index)
-    keep(f4xs, target_x, index_x)
-    for i in (2, 1, 3):
-        device = {"dp": lax.rem(x + i, DPS)}
-        push(f4s, target, index, device)
-        push(f4xs, target_x, index_x, device)
-    sent(spec.at[0, :, pl.ds(0, (DPS - 1) * PIECE)], index)
-    sent(f4x.at[pl.ds(0, DPS - 1)], index_x)
 
     consts[2].wait()
     consts[3].wait()
     send_bs(0, 3)
     rows_forward(0, 0)
     send_bs(1, 0)
+    consts[4].wait()
+    spectrum(0)
     rows_forward(0, 1)
-    spectrum(0)
+    spectrum(1)
     send_bs(1, 1)
     consts[5].wait()
-    await_all(spec.at[0], sem("f4"))
-    await_all(f4x, sem("f4x"))
-    spec_x[0] = f4x[0]
     send_rs(0, times(spec[0], spec[1]), times(spec_x[0], spec_x[1]))
     send_bs(1, 2)
     consts[6].wait()
     rows_back(0, 0)
-    rows_back(0, 1)
     rows_forward(1, 0)
     send_bs(1, 3)
+    rows_back(0, 1)
     send_ds(0, 0)
     send_ds(0, 1)
     rows_forward(1, 1)
+    spectrum(2)
+
+    out_r, out_i = cols_back(conj_times(spec[1], spec[2]), conj_times(spec_x[1], spec_x[2]), first)
+    t4s[0] = out_r
+    t4s[1] = out_i
+    index = over_x("t4", lambda to: t4s.at[:, :, wide(to)], t4.at[x])
+    sent(t4.at[pl.ds(0, DPS - 1)], index)
+
     send_ds(0, 2)
+    send_rs(1, conj_times(spec[0], spec[2]), conj_times(spec_x[0], spec_x[2]))
     send_ds(0, 3)
-    spectrum(1)
-
-    t4s[...] = conj_times(spec[1], spec[2])
-    t4xs[...] = conj_times(spec_x[1], spec_x[2])
-    index, index_x = sem("t4"), sem("t4x")
-    keep(t4s.at[:, rows(x, PIECE)], t4.at[x], index)
-    keep(t4xs, t4x.at[x], index_x)
-    for i in (2, 1, 3):
-        to = lax.rem(x + i, DPS)
-        push(t4s.at[:, rows(to, PIECE)], t4.at[x], index, {"dp": to})
-        push(t4xs, t4x.at[x], index_x, {"dp": to})
-    sent(t4.at[pl.ds(0, DPS - 1)], index)
-    sent(t4x.at[pl.ds(0, DPS - 1)], index_x)
-
-    send_rs(1, conj_times(spec[0], spec[2]), conj_times(spec_x[0], spec_x[2]))
     rows_back(1, 0)
     rows_back(1, 1)
-
+    send_ds(1, 0)
+
+    send_ds(1, 1)
     await_all(t4, sem("t4"))
-    await_all(t4x, sem("t4x"))
-    out_r, out_i = cols_back(
-        t4[0] + t4[1] + t4[2] + t4[3], t4x[0] + t4x[1] + t4x[2] + t4x[3], special
-    )
-    t3s[0] = out_r
-    t3s[1] = out_i
-    index = over_z("t3", lambda z_to: t3s.at[:, :, lanes(z_to)], t3.at[zid])
-    sent(t3.at[pl.ds(0, ZS - 1)], index)
-    send_ds(1, 0)
-    send_ds(1, 1)
-
-    await_all(t3, sem("t3"))
-    t5s[...] = jnp.sum(t3[...], axis=0)
-    index = sem("t5")
-    target = t5.at[:, rows(mine, PIECE)]
-    keep(t5s, target, index)
-    push(t5s, target, index, at_slab(y * 2 + mate))
-    for i in (2, 1, 3):
-        to = lax.rem(x + i, DPS)
-        push(t5s, target, index, {"dp": to})
-        push(t5s, target, index, {"dp": to, **at_slab(y * 2 + mate)})
-    sent(t5.at[:, pl.ds(0, LINES - PIECE)], index)
-    send_ds(1, 2)
-    send_ds(1, 3)
-
-    await_all(t5, sem("t5"))
-    real, imag = t5[0], t5[1]
+    real, imag = t4[0, 0] + t4[1, 0] + t4[2, 0] + t4[3, 0], t4[0, 1] + t4[1, 1] + t4[2, 1] + t4[3, 1]
     cos, sin = turn_f[0], turn_f[1]
-    high, low = split(jnp.concatenate([real * cos - imag * sin, imag * cos + real * sin], axis=0))
+    re, im = real * cos - imag * sin, imag * cos + real * sin
+    low_half = core == 0
+    stacked = [jnp.where(low_half, re, 0.0), jnp.where(low_half, 0.0, re)]
+    stacked += [jnp.where(low_half, im, 0.0), jnp.where(low_half, 0.0, im)]
+    high, low = split(jnp.concatenate(stacked, axis=0))
     both = dot(rows_out[0], high) + dot(rows_out[0], low) + dot(rows_out[1], high)
     t2s[0] = both[:LINES]
     t2s[1] = both[LINES:]
-    index = sem("t2")
-    target = t2.at[pl.ds(y * 2, 2)]
-    keep(t2s.at[:, rows(slab, ROWS)], target, index)
-    for dy in (2, 1, 3):
-        slab_to = lax.rem(y + dy, CHIPS) * 2 + core
-        push(t2s.at[:, rows(slab_to, ROWS)], target, index, at_slab(slab_to))
-    sent(t2.at[pl.ds(0, 2 * (CHIPS - 1))], index)
-
+    index = over_slabs("t2", lambda to: t2s.at[:, rows(to, ROWS)], t2.at[core, pl.ds(y * 2, 2)])
+    sent(t2s.at[:, pl.ds(0, (SLABS - 1) * ROWS)], index)
     await_all(t2, sem("t2"))
-    for i, value in enumerate(blocks_back([t2[u] for u in range(8)])):
+    for i, value in enumerate(blocks_back([t2[0, u] + t2[1, u] for u in range(8)])):
         t1s[i] = value
-    index = over_z("t1", lambda z_to: t1s.at[z_to], t1.at[:, lanes(zid)])
-    sent(t1.at[:, pl.ds(0, SIDE - LANES)], index)
-
-    for a, ref in enumerate([conv_ref, back_ref]):
-        for k in range(CHUNKS):
-            await_all(got_d.at[a, :, :, pl.ds(k * WIDTH, WIDTH)], sem(("d", a * CHUNKS + k)))
-        ref[...] = got_d[a]
+    index = over_z("t1", lambda z_to: t1s.at[z_to], t1.at[zid])
+    sent(t1.at[pl.ds(0, ZS - 1)], index)
+    send_ds(1, 2)
+    send_ds(1, 3)
     await_all(t1, sem("t1"))
-    d_taps_ref[...] = t1[...]
+    t0s[...] = jnp.sum(t1[...], axis=0)
+    index = over_x("t0", lambda to: t0s, t0.at[:, wide(x)])
+    sent(t0.at[:, pl.ds(0, SIDE - WIDTH)], index)
+
+    for k in range(CHUNKS):
+        at = slice(k * WIDTH, (k + 1) * WIDTH)
+        await_all(got_d.at[0, :, :, pl.ds(k * WIDTH, WIDTH)], sem(("d", k)))
+        d_outer_ref[:, :, at] = (grad_ref[:, :, at].astype(F32) * got_d[0, :, :, at]).astype(BF16)
+    for k in range(CHUNKS):
+        at = slice(k * WIDTH, (k + 1) * WIDTH)
+        await_all(got_d.at[1, :, :, pl.ds(k * WIDTH, WIDTH)], sem(("d", CHUNKS + k)))
+        value = got_d[1, :, :, at]
+        d_inner_ref[:, :, at] = (value * signal_ref[:, :, at].astype(F32)).astype(BF16)
+        d_signal_ref[:, :, at] = (value * inner_ref[:, :, at].astype(F32)).astype(BF16)
+    await_all(t0, sem("t0"))
+    d_taps_ref[...] = t0[...]
 
     for ref, index in pending:
         pltpu.make_async_copy(ref, ref, send_sem.at[index]).wait()
@@ -540,11 +526,10 @@
             pltpu.make_async_copy(ref, ref, send_sem.at[sem(("b", a * 2 + i))]).wait()
 
 
-def finish(conv_ref, back_ref, taps_in, grad_ref, signal_ref, inner_ref, outer_out, inner_out, signal_out, taps_out):
-    outer_out[...] = (grad_ref[...].astype(F32) * conv_ref[...]).astype(BF16)
-    inner_out[...] = (back_ref[...] * signal_ref[...].astype(F32)).astype(BF16)
-    signal_out[...] = (back_ref[...] * inner_ref[...].astype(F32)).astype(BF16)
-    taps_out[...] = taps_in[...]
+def finish(*refs):
+    count = len(refs) // 2
+    for i in range(count):
+        refs[count + i][...] = refs[i][...]
 
 
 def shards(consts, outer_gate, inner_gate, signal, grad_out, filter_weight):
@@ -553,13 +538,13 @@
     vmem = pl.BlockSpec(memory_space=pltpu.VMEM)
     anywhere = pl.BlockSpec(memory_space=pl.ANY)
     floats = [
-        (2, LINES, LANES),
+        (2, KROWS, WIDTH),
         (2, ZS, ROWS, SIDE),
         (2, ZS, ROWS, SIDE),
         (2, 8, ROWS, SIDE),
         (2, 2, 2, LINES, WIDTH),
         (2, 2, 2, LINES, WIDTH),
-        (2, 2, KROWS, SIDE),
+        (3, 2, KROWS, SIDE),
         (3, RADIX, KROWS, 2 * QUARTER),
         (3, 8, 2 * QUARTER),
         (2, 2, KROWS, SIDE),
@@ -568,37 +553,30 @@
         (2, 8, ROWS, SIDE),
         (2, ZS, ROWS, SIDE),
         (2, ZS, ROWS, SIDE),
-        (ZS, ROWS, LANES),
-        (8, ROWS, LANES),
-        (2, LINES, LANES),
-        (2, PIECE, LANES),
-        (2, PIECE, SIDE),
-        (RADIX, PIECE, 2 * QUARTER),
-        (8, 2 * QUARTER),
-        (DPS, 8, 2 * QUARTER),
-        (RADIX, KROWS, 2 * QUARTER),
-        (DPS, RADIX, PIECE, 2 * QUARTER),
-        (8, 2 * QUARTER),
-        (DPS, 8, 2 * QUARTER),
-        (2, PIECE, SIDE),
-        (ZS, 2, PIECE, LANES),
-        (2, PIECE, LANES),
-        (2, LINES, LANES),
-        (2, LINES, LANES),
-        (8, ROWS, LANES),
-        (ZS, ROWS, LANES),
+        (ZS, ROWS, WIDTH),
+        (8, ROWS, WIDTH),
+        (2, LINES, WIDTH),
+        (2, KROWS, WIDTH),
+        (2, KROWS, SIDE),
+        (DPS, 2, KROWS, WIDTH),
+        (2, LINES, WIDTH),
+        (2, 8, ROWS, WIDTH),
+        (ZS, ROWS, WIDTH),
+        (ZS, ROWS, WIDTH),
+        (ROWS, WIDTH),
         (ROWS, SIDE),
     ]
-    conv, back, d_taps = pl.pallas_call(
+    results = [jax.ShapeDtypeStruct(shape, BF16)] * 3
+    results += [jax.ShapeDtypeStruct(filter_weight.shape, F32)]
+    outs = pl.pallas_call(
         kernel,
-        out_shape=[
-            jax.ShapeDtypeStruct(shape, F32),
-            jax.ShapeDtypeStruct(shape, F32),
-            jax.ShapeDtypeStruct(filter_weight.shape, F32),
-        ],
-        in_specs=[vmem] * 7 + [anywhere] * 5,
-        out_specs=[vmem] * 3,
-        scratch_shapes=[
+        out_shape=results,
+        in_specs=[anywhere] * 12,
+        out_specs=[vmem] * 4,
+        scratch_shapes=[pltpu.VMEM(shape, BF16)] * 4
+        + [pltpu.VMEM(filter_weight.shape, F32)]
+        + [pltpu.VMEM(twist.shape, F32), pltpu.VMEM(shift.shape, F32)]
+        + [
             pltpu.VMEM(rows_in.shape[1:], BF16),
             pltpu.VMEM(rows_out.shape[1:], BF16),
             pltpu.VMEM(cols_in.shape, BF16),
@@ -607,6 +585,7 @@
         ]
         + [pltpu.VMEM(size, F32) for size in floats]
         + [
+            pltpu.SemaphoreType.DMA((7,)),
             pltpu.SemaphoreType.DMA((7,)),
             pltpu.SemaphoreType.DMA((56,)),
             pltpu.SemaphoreType.DMA((56,)),
@@ -620,11 +599,10 @@
     )
     outs = pl.pallas_call(
         finish,
-        out_shape=[jax.ShapeDtypeStruct(shape, BF16)] * 3
-        + [jax.ShapeDtypeStruct(filter_weight.shape, F32)],
-        in_specs=[vmem] * 6,
+        out_shape=results,
+        in_specs=[vmem] * 4,
         out_specs=[vmem] * 4,
-    )(conv, back, d_taps, grad_out[0], signal[0], inner_gate[0])
+    )(*outs)
     return outs[0][None], outs[1][None], outs[2][None], outs[3]
 
 

time: 82.2 us -> 75.5 us (0.918)
  Pallas kernels: 81.4 us -> 74.8 us
    pallas_call x2, Pallas kernels: 81.4 us -> 74.8 us  [the longest x1 72.8 us: shards(): pl.pallas_call(kernel, out_shape=results, in_specs=[anywhere] * 12, out_s...]
where the time goes in v3:
time: 75.5 us; the launch traced here: 75.4 us
  Pallas kernels  74.8 us (99%)
    pallas_call x1, Pallas kernels, shards(): pl.pallas_call(kernel, out_shape=results, in_specs=[anywhere] * 12, out_s...  72.8 us
    pallas_call x1, Pallas kernels, shards(): pl.pallas_call(finish, out_shape=results, in_specs=[vmem] * 4, out_specs=...  2.02 us

profile of v3, /device:TPU:1, one launch (start us, length us, event | category | flops | bytes accessed | tf_op | source)
XLA Modules:
  0.0 75.4 jit_solution(9058378390186281972)
XLA Ops:
  0.6 72.8 %shard_map.147 = (bf16[8,16,1024]{2,1,0:T(8,128)(2,1)}, bf16[8,16,1024]{2,1,0:T(8,128)(2,1)}, bf16[8,16,1024]{2,1,0:T(8,128)(2,1)}, f32[16,1024]{1,0:T(8,128)}) custom-call(bf16[8,16,1024]{2,1,0:T(8,128)(2,1)} %bitcast.7, bf16[8,16,1024]{2,1,0:T(8,128)(2,1)} %bitcast.8, bf16[8,16,1024]{2,1,0:T(8,128)(2,1)} %bitcast.9, bf16[8,16,1024]{2,1,0:T(8,128)(2,1)} %bitcast.10, ...), custom_call_target="tpu_custom_call" | custom-call | tf_op jit(solution)/shard_map/pallas_call | solution.py:571
  73.4 2.0 %shard_map.148 = (bf16[8,16,1024]{2,1,0:T(8,128)(2,1)}, bf16[8,16,1024]{2,1,0:T(8,128)(2,1)}, bf16[8,16,1024]{2,1,0:T(8,128)(2,1)}, f32[16,1024]{1,0:T(8,128)}) custom-call(bf16[8,16,1024]{2,1,0:T(8,128)(2,1)} %get-tuple-element.12.refs_0_, bf16[8,16,1024]{2,1,0:T(8,128)(2,1)} %get-tuple-element.13.refs_1_, bf16[8,16,1024]{2,1,0:T(8,128)(2,1)} %get-tuple-element.14.refs_2_, ...), custom_call_target="tpu_custom_call" | custom-call | tf_op jit(solution)/shard_map/pallas_call | solution.py:600

commit v4 on v3

--- a/solution.py
+++ b/solution.py
@@ -155,7 +155,7 @@
         copy.start()
 
     barrier = pltpu.get_barrier_semaphore()
-    order = (4, 3, 5, 2, 6, 1, 7)
+    order = (4, 5, 3, 6, 2, 7, 1)
     partners = [at_z(i)[1] for i in order]
     partners += [at_slab(lax.rem(slab + i, SLABS)) for i in range(1, SLABS)]
     for i in range(1, DPS):
@@ -179,10 +179,7 @@
     ]
     for copy in consts:
         copy.start()
-    for copy in inputs:
-        copy.wait()
-    gated[0] = inner_ref[...].astype(F32) * signal_ref[...].astype(F32)
-    gated[1] = grad_ref[...].astype(F32) * outer_ref[...].astype(F32)
+    inputs[0].wait()
     pl.semaphore_wait(barrier, len(partners))
 
     names = {}
@@ -239,6 +236,9 @@
         return index
 
     def send_a(a, k):
+        left, right = [(inner_ref, signal_ref), (grad_ref, outer_ref)][a]
+        at = slice(k * WIDTH, (k + 1) * WIDTH)
+        gated[a, :, :, at] = left[:, :, at].astype(F32) * right[:, :, at].astype(F32)
         at = pl.ds(k * WIDTH, WIDTH)
         index = over_z(
             ("a", a * CHUNKS + k), lambda z_to: gated.at[a, z_to, :, at], got_a.at[a, zid, :, at]
@@ -411,6 +411,8 @@
 
     index = over_z("f1", lambda z_to: taps_ref.at[:, wide(x)], f1.at[zid])
     sent(f1.at[pl.ds(0, ZS - 1)], index)
+    inputs[1].wait()
+    inputs[2].wait()
     for k in range(CHUNKS):
         send_a(0, k)
 
@@ -437,6 +439,8 @@
     index = over_x(("q", 0), lambda to: f3s, got_q.at[0, :, :, wide(x)])
     sent(got_q.at[0, :, :, pl.ds(0, SIDE - WIDTH)], index)
 
+    for copy in inputs[3:]:
+        copy.wait()
     for k in range(CHUNKS):
         send_a(1, k)
     send_bs(0, 0)
@@ -451,8 +455,8 @@
     consts[4].wait()
     spectrum(0)
     rows_forward(0, 1)
+    send_bs(1, 1)
     spectrum(1)
-    send_bs(1, 1)
     consts[5].wait()
     send_rs(0, times(spec[0], spec[1]), times(spec_x[0], spec_x[1]))
     send_bs(1, 2)
@@ -461,9 +465,9 @@
     rows_forward(1, 0)
     send_bs(1, 3)
     rows_back(0, 1)
+    rows_forward(1, 1)
     send_ds(0, 0)
     send_ds(0, 1)
-    rows_forward(1, 1)
     spectrum(2)
 
     out_r, out_i = cols_back(conj_times(spec[1], spec[2]), conj_times(spec_x[1], spec_x[2]), first)
@@ -472,14 +476,12 @@
     index = over_x("t4", lambda to: t4s.at[:, :, wide(to)], t4.at[x])
     sent(t4.at[pl.ds(0, DPS - 1)], index)
 
+    send_rs(1, conj_times(spec[0], spec[2]), conj_times(spec_x[0], spec_x[2]))
     send_ds(0, 2)
-    send_rs(1, conj_times(spec[0], spec[2]), conj_times(spec_x[0], spec_x[2]))
+    rows_back(1, 0)
     send_ds(0, 3)
-    rows_back(1, 0)
     rows_back(1, 1)
     send_ds(1, 0)
-
-    send_ds(1, 1)
     await_all(t4, sem("t4"))
     real, imag = t4[0, 0] + t4[1, 0] + t4[2, 0] + t4[3, 0], t4[0, 1] + t4[1, 1] + t4[2, 1] + t4[3, 1]
     cos, sin = turn_f[0], turn_f[1]
@@ -493,6 +495,7 @@
     t2s[1] = both[LINES:]
     index = over_slabs("t2", lambda to: t2s.at[:, rows(to, ROWS)], t2.at[core, pl.ds(y * 2, 2)])
     sent(t2s.at[:, pl.ds(0, (SLABS - 1) * ROWS)], index)
+    send_ds(1, 1)
     await_all(t2, sem("t2"))
     for i, value in enumerate(blocks_back([t2[0, u] + t2[1, u] for u in range(8)])):
         t1s[i] = value

time: 75.5 us -> 74.8 us (level)
  Pallas kernels: 74.8 us -> 74 us
    pallas_call x1, Pallas kernels: 72.8 us -> 72 us  [shards(): pl.pallas_call(kernel, out_shape=results, in_specs=[anywhere] * 12, out_s...]
where the time goes in v4:
time: 74.8 us; the launch traced here: 74.7 us
  Pallas kernels  74 us (99%)
    pallas_call x1, Pallas kernels, shards(): pl.pallas_call(kernel, out_shape=results, in_specs=[anywhere] * 12, out_s...  72 us
    pallas_call x1, Pallas kernels, shards(): pl.pallas_call(finish, out_shape=results, in_specs=[vmem] * 4, out_specs=...  2.02 us

profile of v4, /device:TPU:1, one launch (start us, length us, event | category | flops | bytes accessed | tf_op | source)
XLA Modules:
  0.0 74.7 jit_solution(6983994681536199657)
XLA Ops:
  0.6 72.0 %shard_map.147 = (bf16[8,16,1024]{2,1,0:T(8,128)(2,1)}, bf16[8,16,1024]{2,1,0:T(8,128)(2,1)}, bf16[8,16,1024]{2,1,0:T(8,128)(2,1)}, f32[16,1024]{1,0:T(8,128)}) custom-call(bf16[8,16,1024]{2,1,0:T(8,128)(2,1)} %bitcast.7, bf16[8,16,1024]{2,1,0:T(8,128)(2,1)} %bitcast.8, bf16[8,16,1024]{2,1,0:T(8,128)(2,1)} %bitcast.9, bf16[8,16,1024]{2,1,0:T(8,128)(2,1)} %bitcast.10, ...), custom_call_target="tpu_custom_call" | custom-call | tf_op jit(solution)/shard_map/pallas_call | solution.py:574
  72.6 2.0 %shard_map.148 = (bf16[8,16,1024]{2,1,0:T(8,128)(2,1)}, bf16[8,16,1024]{2,1,0:T(8,128)(2,1)}, bf16[8,16,1024]{2,1,0:T(8,128)(2,1)}, f32[16,1024]{1,0:T(8,128)}) custom-call(bf16[8,16,1024]{2,1,0:T(8,128)(2,1)} %get-tuple-element.12.refs_0_, bf16[8,16,1024]{2,1,0:T(8,128)(2,1)} %get-tuple-element.13.refs_1_, bf16[8,16,1024]{2,1,0:T(8,128)(2,1)} %get-tuple-element.14.refs_2_, ...), custom_call_target="tpu_custom_call" | custom-call | tf_op jit(solution)/shard_map/pallas_call | solution.py:603

commit v5 on v4

--- a/solution.py
+++ b/solution.py
@@ -106,12 +106,13 @@
 def kernel(
     outer_hbm, inner_hbm, signal_hbm, grad_hbm, taps_hbm, twist_hbm, shift_hbm,
     rows_in_hbm, rows_out_hbm, cols_in_hbm, cols_out_hbm, turn_hbm,
-    d_outer_ref, d_inner_ref, d_signal_ref, d_taps_ref,
+    d_outer_hbm, d_inner_hbm, d_signal_hbm, d_taps_hbm,
+    d_outer_ref, d_inner_ref, d_signal_ref,
     outer_ref, inner_ref, signal_ref, grad_ref, taps_ref, twist_ref, shift_ref,
     rows_in, rows_out, cols_in, cols_out, turn, turn_f,
     gated, got_a, send_b, got_b, send_q, got_q, spec, spec_x, send_r, got_r, send_c, got_c, done, got_d,
     f1, f2s, f2, f3s, t4s, t4, t2s, t2, t1s, t1, t0s, t0,
-    input_sem, const_sem, send_sem, recv_sem,
+    input_sem, const_sem, out_sem, send_sem, recv_sem,
 ):
     x = lax.axis_index("dp")
     row = lax.axis_index("row")
@@ -508,18 +509,28 @@
     index = over_x("t0", lambda to: t0s, t0.at[:, wide(x)])
     sent(t0.at[:, pl.ds(0, SIDE - WIDTH)], index)
 
+    written = []
+
+    def write(source, target):
+        copy = pltpu.make_async_copy(source, target, out_sem.at[len(written)])
+        copy.start()
+        written.append(copy)
+
     for k in range(CHUNKS):
-        at = slice(k * WIDTH, (k + 1) * WIDTH)
-        await_all(got_d.at[0, :, :, pl.ds(k * WIDTH, WIDTH)], sem(("d", k)))
+        at = pl.ds(k * WIDTH, WIDTH)
+        await_all(got_d.at[0, :, :, at], sem(("d", k)))
         d_outer_ref[:, :, at] = (grad_ref[:, :, at].astype(F32) * got_d[0, :, :, at]).astype(BF16)
+    write(d_outer_ref, d_outer_hbm)
     for k in range(CHUNKS):
-        at = slice(k * WIDTH, (k + 1) * WIDTH)
-        await_all(got_d.at[1, :, :, pl.ds(k * WIDTH, WIDTH)], sem(("d", CHUNKS + k)))
+        at = pl.ds(k * WIDTH, WIDTH)
+        await_all(got_d.at[1, :, :, at], sem(("d", CHUNKS + k)))
         value = got_d[1, :, :, at]
         d_inner_ref[:, :, at] = (value * signal_ref[:, :, at].astype(F32)).astype(BF16)
         d_signal_ref[:, :, at] = (value * inner_ref[:, :, at].astype(F32)).astype(BF16)
+        write(d_inner_ref.at[:, :, at], d_inner_hbm.at[:, :, at])
+        write(d_signal_ref.at[:, :, at], d_signal_hbm.at[:, :, at])
     await_all(t0, sem("t0"))
-    d_taps_ref[...] = t0[...]
+    write(t0, d_taps_hbm)
 
     for ref, index in pending:
         pltpu.make_async_copy(ref, ref, send_sem.at[index]).wait()
@@ -527,6 +538,8 @@
         for i in range(2):
             ref = got_b.at[a, i, :, pl.ds(0, (SLABS - 1) * ROWS)]
             pltpu.make_async_copy(ref, ref, send_sem.at[sem(("b", a * 2 + i))]).wait()
+    for copy in written:
+        copy.wait()
 
 
 def finish(*refs):
@@ -575,8 +588,8 @@
         kernel,
         out_shape=results,
         in_specs=[anywhere] * 12,
-        out_specs=[vmem] * 4,
-        scratch_shapes=[pltpu.VMEM(shape, BF16)] * 4
+        out_specs=[anywhere] * 4,
+        scratch_shapes=[pltpu.VMEM(shape, BF16)] * 7
         + [pltpu.VMEM(filter_weight.shape, F32)]
         + [pltpu.VMEM(twist.shape, F32), pltpu.VMEM(shift.shape, F32)]
         + [
@@ -590,6 +603,7 @@
         + [
             pltpu.SemaphoreType.DMA((7,)),
             pltpu.SemaphoreType.DMA((7,)),
+            pltpu.SemaphoreType.DMA((2 + 2 * CHUNKS,)),
             pltpu.SemaphoreType.DMA((56,)),
             pltpu.SemaphoreType.DMA((56,)),
         ],

time: 74.8 us -> 74.6 us (level)
  no operation moved by 1% of the time
where the time goes in v5:
time: 74.6 us; the launch traced here: 74.5 us
  Pallas kernels  73.8 us (99%)
    pallas_call x1, Pallas kernels, shards(): pl.pallas_call(kernel, out_shape=results, in_specs=[anywhere] * 12, out_s...  71.8 us
    pallas_call x1, Pallas kernels, shards(): pl.pallas_call(finish, out_shape=results, in_specs=[vmem] * 4, out_specs=...  2.02 us

profile of v5, /device:TPU:1, one launch (start us, length us, event | category | flops | bytes accessed | tf_op | source)
XLA Modules:
  0.0 74.5 jit_solution(11692634945055179084)
XLA Ops:
  0.6 71.8 %shard_map.147 = (bf16[8,16,1024]{2,1,0:T(8,128)(2,1)}, bf16[8,16,1024]{2,1,0:T(8,128)(2,1)}, bf16[8,16,1024]{2,1,0:T(8,128)(2,1)}, f32[16,1024]{1,0:T(8,128)}) custom-call(bf16[8,16,1024]{2,1,0:T(8,128)(2,1)} %bitcast.7, bf16[8,16,1024]{2,1,0:T(8,128)(2,1)} %bitcast.8, bf16[8,16,1024]{2,1,0:T(8,128)(2,1)} %bitcast.9, bf16[8,16,1024]{2,1,0:T(8,128)(2,1)} %bitcast.10, ...), custom_call_target="tpu_custom_call" | custom-call | tf_op jit(solution)/shard_map/pallas_call | solution.py:587
  72.4 2.0 %shard_map.148 = (bf16[8,16,1024]{2,1,0:T(8,128)(2,1)}, bf16[8,16,1024]{2,1,0:T(8,128)(2,1)}, bf16[8,16,1024]{2,1,0:T(8,128)(2,1)}, f32[16,1024]{1,0:T(8,128)}) custom-call(bf16[8,16,1024]{2,1,0:T(8,128)(2,1)} %get-tuple-element.12.refs_0_, bf16[8,16,1024]{2,1,0:T(8,128)(2,1)} %get-tuple-element.13.refs_1_, bf16[8,16,1024]{2,1,0:T(8,128)(2,1)} %get-tuple-element.14.refs_2_, ...), custom_call_target="tpu_custom_call" | custom-call | tf_op jit(solution)/shard_map/pallas_call | solution.py:617
